TPU v7x, 32 devices: a whole 2x2x4 slice. The times are simulated.
32 devices in a mesh: dp: 4 (over x, core), ctx: 4 (over z), exp: 2 (over y).
Axes of the slice: x: 2, y: 2, z: 4, core: 2. Of those that a mesh axis runs over, the one named last changes fastest.
Arguments:
- block_input: bfloat16 [8, 1024, 768], P(('dp', 'exp'), 'ctx'), may hold values from -6 to 6
- out_cotangent: bfloat16 [8, 1024, 768], P(('dp', 'exp'), 'ctx'), may hold values from -6 to 6
- expert_ids: int32 [2, 8, 4, 256, 1], P(None, ('dp', 'exp'), 'ctx'), may hold values from 0 to 3; in each aligned block of 256 rows (0 to 255, 256 to 511, ..., all dimensions but the last counted through in order) at most 128 rows name the same one
- rel_buckets: int32 [2047], replicated, may hold values from 0 to 31
- bias_table: bfloat16 [32, 12], replicated, may hold values from -6 to 6
- gain_attn: bfloat16 [2, 768], P(None, 'dp'), may hold values from 0.5 to 1.5
- w_query: bfloat16 [2, 768, 768], P(None, 'dp'), may hold values from -0.21875 to 0.21875
- w_key: bfloat16 [2, 768, 768], P(None, 'dp'), may hold values from -0.21875 to 0.21875
- w_value: bfloat16 [2, 768, 768], P(None, 'dp'), may hold values from -0.21875 to 0.21875
- w_output: bfloat16 [2, 768, 768], P(None, 'dp'), may hold values from -3.5 to 3.5
- gain_ffn: bfloat16 [2, 768], P(None, 'dp'), may hold values from 0.5 to 1.5
- w_router: bfloat16 [2, 768, 4], P(None, 'dp'), may hold values from -0.109375 to 0.109375
- w_inner: bfloat16 [2, 4, 768, 3072], P(None, 'exp', 'dp'), may hold values from -0.21875 to 0.21875
- w_outer: bfloat16 [2, 4, 3072, 768], P(None, 'exp', 'dp'), may hold values from -0.75 to 0.75
Outputs:
- block_output: bfloat16 [8, 1024, 768], P(('dp', 'exp'), 'ctx')
- input_grad: float32 [8, 1024, 768], P(('dp', 'exp'), 'ctx')
- gain_attn_grad: float32 [2, 768], P(None, 'dp')
- w_query_grad: float32 [2, 768, 768], P(None, 'dp')
- w_key_grad: float32 [2, 768, 768], P(None, 'dp')
- w_value_grad: float32 [2, 768, 768], P(None, 'dp')
- w_output_grad: float32 [2, 768, 768], P(None, 'dp')
- gain_ffn_grad: float32 [2, 768], P(None, 'dp')
- w_router_grad: float32 [2, 768, 4], P(None, 'dp')
- w_inner_grad: float32 [2, 4, 768, 3072], P(None, 'exp', 'dp')
- w_outer_grad: float32 [2, 4, 3072, 768], P(None, 'exp', 'dp')
- bias_table_grad: float32 [32, 12], P(None, 'dp')
Inputs may be any that keep to these rules, and one draw needn't show every extreme that they name: `expert_ids`: row r of group (g, c) is token r % 256 of block c of sequence g + r // 256. In each layer no expert is named by more than 128 of the rows of one group (g, c), a bound that some group reaches. `rel_buckets`: entry 1023 + j - i is the bucket of key position j seen from query position i.
All inputs are finite; a program needn't handle non-finite values.
Results may differ from a plain program's by a relative error of at most 0.035.
Values may be sent and summed in bfloat16 or wider, within the bound.
A program may use at most 320 MiB of HBM per device.

v0:
```python
from functools import partial

import jax
import jax.numpy as jnp
from jax import lax
from jax.sharding import PartitionSpec as P

NORM_EPSILON = 1e-06
PRECISION_HIGH = lax.Precision.HIGHEST


def passed_along(block, axis, distance):
    devices = range(lax.axis_size(axis))
    route = [((i - distance) % len(devices), i) for i in devices]
    return lax.ppermute(block, axis, route)


def rms_norm(values, gain):
    return (
        values * lax.rsqrt(jnp.mean(values * values, axis=-1, keepdims=True) + NORM_EPSILON) * gain
    )


def head_split(values, head_count):
    return values.reshape(
        values.shape[0], values.shape[1], head_count, values.shape[2] // head_count
    )


def head_merge(values):
    return values.reshape(values.shape[0], values.shape[1], values.shape[2] * values.shape[3])


def bucket_onehot(rel_buckets, offset_blocks, block_len, bucket_count):
    half_span = (rel_buckets.shape[0] + 1) // 2
    seg_start = offset_blocks * block_len + half_span - block_len
    segment = lax.dynamic_slice_in_dim(rel_buckets, seg_start, 2 * block_len - 1)
    widened = jnp.broadcast_to(segment[None, :], (block_len, 2 * block_len - 1)).reshape(
        block_len * (2 * block_len - 1)
    )
    skewed = widened[block_len - 1 : block_len - 1 + block_len * (2 * block_len - 2)].reshape(
        block_len, 2 * block_len - 2
    )
    tile = skewed[:, :block_len]
    return (tile[:, :, None] == jnp.arange(bucket_count, dtype=jnp.int32)[None, None, :]).astype(
        jnp.float32
    )


def bias_from_onehot(onehot, table_full):
    return jnp.einsum("qkb,bh->hqk", onehot, table_full, precision=PRECISION_HIGH)


def slot_targets(expert_row, experts_all, capacity):
    onehot = (expert_row[:, None] == jnp.arange(experts_all, dtype=jnp.int32)[None, :]).astype(
        jnp.int32
    )
    rank_before = jnp.cumsum(onehot, axis=0) - onehot
    return expert_row * capacity + jnp.sum(rank_before * onehot, axis=1)


def cycle_forward(query_low, key_low, value_low, table_full, rel_buckets, head_count):
    ctx_count = lax.axis_size("ctx")
    ctx_index = lax.axis_index("ctx")
    seq_count, block_len, hidden = query_low.shape
    bucket_count = table_full.shape[0]
    score_scale = (hidden // head_count) ** (-0.5)
    query_heads = head_split(query_low, head_count)

    def absorb(softmax_stats, key_blk, value_blk, anchor):
        run_max, run_sum, accum = softmax_stats
        raw_scores = jnp.einsum(
            "sqhd,skhd->shqk",
            query_heads,
            head_split(key_blk, head_count),
            preferred_element_type=jnp.float32,
        )
        onehot = bucket_onehot(rel_buckets, anchor - ctx_index, block_len, bucket_count)
        scores = raw_scores * score_scale + bias_from_onehot(onehot, table_full)[None]
        new_max = jnp.maximum(run_max, jnp.max(scores, axis=-1))
        weights = jnp.exp(scores - new_max[..., None])
        shrink = jnp.exp(run_max - new_max)
        partial_out = jnp.einsum(
            "shqk,skhd->sqhd",
            weights.astype(jnp.bfloat16),
            head_split(value_blk, head_count),
            preferred_element_type=jnp.float32,
        )
        shrink_rows = jnp.transpose(shrink, (0, 2, 1))[..., None]
        return (
            new_max,
            run_sum * shrink + jnp.sum(weights, axis=-1),
            accum * shrink_rows + partial_out,
        )

    initial = (
        jnp.full((seq_count, head_count, block_len), -jnp.inf, jnp.float32),
        jnp.zeros((seq_count, head_count, block_len), jnp.float32),
        jnp.zeros(query_heads.shape, jnp.float32),
    )
    softmax_stats = absorb(initial, key_low, value_low, ctx_index)

    def advance(cycle_step, carry):
        key_blk, value_blk, running = carry
        key_blk, value_blk = passed_along((key_blk, value_blk), "ctx", 1)
        anchor = (ctx_index - cycle_step) % ctx_count
        return (key_blk, value_blk, absorb(running, key_blk, value_blk, anchor))

    carry = lax.fori_loop(1, ctx_count, advance, (key_low, value_low, softmax_stats))
    run_max, run_sum, accum = carry[2]
    out_full = head_merge(accum / jnp.transpose(run_sum, (0, 2, 1))[..., None])
    return (out_full, run_max + jnp.log(run_sum))


def cycle_backward(
    query_low, key_low, value_low, out_full, mix_grad, log_norm, table_full, rel_buckets, head_count
):
    ctx_count = lax.axis_size("ctx")
    ctx_index = lax.axis_index("ctx")
    seq_count, block_len, hidden = query_low.shape
    bucket_count = table_full.shape[0]
    score_scale = (hidden // head_count) ** (-0.5)
    query_heads = head_split(query_low, head_count)
    grad_heads = head_split(mix_grad, head_count)
    row_delta = jnp.transpose(
        jnp.sum(head_split(mix_grad.astype(jnp.float32) * out_full, head_count), axis=-1), (0, 2, 1)
    )

    def advance(cycle_step, carry):
        key_blk, value_blk, key_grad, value_grad, query_grad, table_grad = carry
        anchor = (ctx_index - cycle_step) % ctx_count
        key_heads = head_split(key_blk, head_count)
        value_heads = head_split(value_blk, head_count)
        onehot = bucket_onehot(rel_buckets, anchor - ctx_index, block_len, bucket_count)
        bias_block = bias_from_onehot(onehot, table_full)
        raw_scores = jnp.einsum(
            "sqhd,skhd->shqk", query_heads, key_heads, preferred_element_type=jnp.float32
        )
        probabilities = jnp.exp(raw_scores * score_scale + bias_block[None] - log_norm[..., None])
        prob_grad = jnp.einsum(
            "sqhd,skhd->shqk", grad_heads, value_heads, preferred_element_type=jnp.float32
        )
        score_grad = probabilities * (prob_grad - row_delta[..., None])
        table_grad = table_grad + jnp.einsum(
            "hqk,qkb->bh", jnp.sum(score_grad, axis=0), onehot, precision=PRECISION_HIGH
        )
        scaled = (score_grad * score_scale).astype(jnp.bfloat16)
        query_grad = query_grad + jnp.einsum(
            "shqk,skhd->sqhd", scaled, key_heads, preferred_element_type=jnp.float32
        )
        key_grad = key_grad + jnp.einsum(
            "shqk,sqhd->skhd", scaled, query_heads, preferred_element_type=jnp.float32
        )
        value_grad = value_grad + jnp.einsum(
            "shqk,sqhd->skhd",
            probabilities.astype(jnp.bfloat16),
            grad_heads,
            preferred_element_type=jnp.float32,
        )
        key_blk, value_blk = passed_along((key_blk, value_blk), "ctx", 1)
        key_grad, value_grad = (
            passed_along(key_grad.astype(jnp.bfloat16), "ctx", 1).astype(key_grad.dtype),
            passed_along(value_grad.astype(jnp.bfloat16), "ctx", 1).astype(value_grad.dtype),
        )
        return (key_blk, value_blk, key_grad, value_grad, query_grad, table_grad)

    zeros_heads = jnp.zeros(query_heads.shape, jnp.float32)
    carry = lax.fori_loop(
        0,
        ctx_count,
        advance,
        (
            key_low,
            value_low,
            zeros_heads,
            zeros_heads,
            zeros_heads,
            jnp.zeros(table_full.shape, jnp.float32),
        ),
    )
    return (head_merge(carry[4]), head_merge(carry[2]), head_merge(carry[3]), carry[5])


def layer_forward(
    stream, weights, table_full, rel_buckets, route_row, head_count, experts_all, capacity
):
    (
        gain_one,
        query_weight,
        key_weight,
        value_weight,
        output_weight,
        gain_two,
        router_weight,
        inner_weight,
        outer_weight,
    ) = weights
    seq_count, block_len, model_width = stream.shape
    normed_one = rms_norm(stream, gain_one.astype(jnp.float32)).astype(jnp.bfloat16)
    query_low = jnp.dot(normed_one, query_weight, preferred_element_type=jnp.float32).astype(
        jnp.bfloat16
    )
    key_low = jnp.dot(normed_one, key_weight, preferred_element_type=jnp.float32).astype(
        jnp.bfloat16
    )
    value_low = jnp.dot(normed_one, value_weight, preferred_element_type=jnp.float32).astype(
        jnp.bfloat16
    )
    out_full, log_norm = cycle_forward(
        query_low, key_low, value_low, table_full, rel_buckets, head_count
    )
    mixed_low = out_full.astype(jnp.bfloat16)
    mid_stream = stream + jnp.dot(mixed_low, output_weight, preferred_element_type=jnp.float32)
    normed_two = rms_norm(mid_stream, gain_two.astype(jnp.float32)).astype(jnp.bfloat16)
    rows_two = normed_two.reshape(seq_count * block_len, model_width)
    router_probs = jax.nn.softmax(
        jnp.dot(rows_two, router_weight, preferred_element_type=jnp.float32), axis=-1
    )
    expert_hot = (route_row[:, None] == jnp.arange(experts_all, dtype=jnp.int32)[None, :]).astype(
        jnp.float32
    )
    gate_value = jnp.sum(router_probs * expert_hot, axis=-1, keepdims=True)
    targets = slot_targets(route_row, experts_all, capacity)
    outgoing = (
        jnp.zeros((experts_all * capacity, model_width), jnp.bfloat16).at[targets].set(rows_two)
    )
    received = lax.all_to_all(
        outgoing.reshape(experts_all, capacity, model_width),
        "exp",
        split_axis=0,
        concat_axis=1,
        tiled=True,
    )
    pre_act = jnp.einsum("erd,edf->erf", received, inner_weight, preferred_element_type=jnp.float32)
    activated = jax.nn.gelu(pre_act, approximate=True).astype(jnp.bfloat16)
    expert_out = jnp.einsum(
        "erf,efd->erd", activated, outer_weight, preferred_element_type=jnp.float32
    ).astype(jnp.bfloat16)
    returned = lax.all_to_all(expert_out, "exp", split_axis=1, concat_axis=0, tiled=True).reshape(
        experts_all * capacity, model_width
    )[targets]
    new_stream = mid_stream + (gate_value * returned.astype(jnp.float32)).reshape(stream.shape)
    saved_state = (
        stream,
        normed_one,
        query_low,
        key_low,
        value_low,
        out_full,
        log_norm,
        mixed_low,
        mid_stream,
        normed_two,
        router_probs,
        expert_hot,
        gate_value,
        targets,
        received,
        pre_act,
        activated,
        returned,
    )
    return (new_stream, saved_state)


def layer_backward(
    grad_stream, saved_state, weights, table_full, rel_buckets, head_count, experts_all, capacity
):
    (
        gain_one,
        query_weight,
        key_weight,
        value_weight,
        output_weight,
        gain_two,
        router_weight,
        inner_weight,
        outer_weight,
    ) = weights
    (
        stream,
        normed_one,
        query_low,
        key_low,
        value_low,
        out_full,
        log_norm,
        mixed_low,
        mid_stream,
        normed_two,
        router_probs,
        expert_hot,
        gate_value,
        targets,
        received,
        pre_act,
        activated,
        returned,
    ) = saved_state
    seq_count, block_len, model_width = stream.shape
    rows_grad = grad_stream.reshape(seq_count * block_len, model_width)
    gate_grad = jnp.sum(rows_grad * returned.astype(jnp.float32), axis=-1, keepdims=True)
    out_grad = (gate_value * rows_grad).astype(jnp.bfloat16)
    outgoing = (
        jnp.zeros((experts_all * capacity, model_width), jnp.bfloat16).at[targets].set(out_grad)
    )
    expert_grad = lax.all_to_all(
        outgoing.reshape(experts_all, capacity, model_width),
        "exp",
        split_axis=0,
        concat_axis=1,
        tiled=True,
    )
    outer_grad = jnp.einsum(
        "erf,erd->efd", activated, expert_grad, preferred_element_type=jnp.float32
    )
    act_grad = jnp.einsum(
        "erd,efd->erf", expert_grad, outer_weight, preferred_element_type=jnp.float32
    )
    pre_grad = jax.vjp(partial(jax.nn.gelu, approximate=True), pre_act)[1](act_grad)[0].astype(
        jnp.bfloat16
    )
    inner_grad = jnp.einsum("erd,erf->edf", received, pre_grad, preferred_element_type=jnp.float32)
    token_back = jnp.einsum(
        "erf,edf->erd", pre_grad, inner_weight, preferred_element_type=jnp.float32
    )
    token_back = (
        lax.all_to_all(
            token_back.astype(jnp.bfloat16), "exp", split_axis=1, concat_axis=0, tiled=True
        )
        .astype(token_back.dtype)
        .reshape(experts_all * capacity, model_width)[targets]
    )
    logit_grad = (router_probs * (expert_hot - gate_value) * gate_grad).astype(jnp.bfloat16)
    rows_two = normed_two.reshape(seq_count * block_len, model_width)
    router_grad = jnp.einsum("rd,re->de", rows_two, logit_grad, preferred_element_type=jnp.float32)
    two_grad = (
        jnp.einsum("re,de->rd", logit_grad, router_weight, preferred_element_type=jnp.float32)
        + token_back
    )
    normed_mid, norm_back = jax.vjp(rms_norm, mid_stream, gain_two.astype(jnp.float32))
    mid_part, gain_two_grad = norm_back(two_grad.reshape(stream.shape))
    mid_grad = grad_stream + mid_part
    attn_grad = mid_grad.astype(jnp.bfloat16)
    output_grad = jnp.einsum(
        "sbe,sbd->ed", mixed_low, attn_grad, preferred_element_type=jnp.float32
    )
    mix_grad = jnp.einsum(
        "sbd,ed->sbe", attn_grad, output_weight, preferred_element_type=jnp.float32
    ).astype(jnp.bfloat16)
    query_grad, key_grad, value_grad, table_grad = cycle_backward(
        query_low,
        key_low,
        value_low,
        out_full,
        mix_grad,
        log_norm,
        table_full,
        rel_buckets,
        head_count,
    )
    query_grad = query_grad.astype(jnp.bfloat16)
    key_grad = key_grad.astype(jnp.bfloat16)
    value_grad = value_grad.astype(jnp.bfloat16)
    query_weight_grad = jnp.einsum(
        "sbd,sbe->de", normed_one, query_grad, preferred_element_type=jnp.float32
    )
    key_weight_grad = jnp.einsum(
        "sbd,sbe->de", normed_one, key_grad, preferred_element_type=jnp.float32
    )
    value_weight_grad = jnp.einsum(
        "sbd,sbe->de", normed_one, value_grad, preferred_element_type=jnp.float32
    )
    one_grad = jnp.einsum(
        "sbe,de->sbd", query_grad, query_weight, preferred_element_type=jnp.float32
    )
    one_grad = one_grad + jnp.einsum(
        "sbe,de->sbd", key_grad, key_weight, preferred_element_type=jnp.float32
    )
    one_grad = one_grad + jnp.einsum(
        "sbe,de->sbd", value_grad, value_weight, preferred_element_type=jnp.float32
    )
    normed_in, norm_back_one = jax.vjp(rms_norm, stream, gain_one.astype(jnp.float32))
    stream_part, gain_one_grad = norm_back_one(one_grad)
    attn_terms = (
        gain_one_grad,
        query_weight_grad,
        key_weight_grad,
        value_weight_grad,
        output_grad,
        gain_two_grad,
        router_grad,
    )
    return (mid_grad + stream_part, attn_terms, (inner_grad, outer_grad), table_grad)


def stack_member(layer_parts, position):
    return jnp.stack([layer_part[position] for layer_part in layer_parts])


def shards(
    block_input,
    out_cotangent,
    expert_ids,
    rel_buckets,
    bias_table,
    gain_attn,
    w_query,
    w_key,
    w_value,
    w_output,
    gain_ffn,
    w_router,
    w_inner,
    w_outer,
):
    layer_count = gain_attn.shape[0]
    head_count = bias_table.shape[1]
    experts_all = w_inner.shape[1] * lax.axis_size("exp")
    seq_count, block_len, model_width = block_input.shape
    capacity = 2 * seq_count * block_len // experts_all
    table_full = bias_table.astype(jnp.float32)
    stream = block_input.astype(jnp.float32)
    fetched = []
    kept_states = []
    for layer_id in range(layer_count):
        weights = (
            lax.all_gather(gain_attn[layer_id], "dp", axis=0, tiled=True),
            lax.all_gather(w_query[layer_id], "dp", axis=0, tiled=True),
            lax.all_gather(w_key[layer_id], "dp", axis=0, tiled=True),
            lax.all_gather(w_value[layer_id], "dp", axis=0, tiled=True),
            lax.all_gather(w_output[layer_id], "dp", axis=0, tiled=True),
            lax.all_gather(gain_ffn[layer_id], "dp", axis=0, tiled=True),
            lax.all_gather(w_router[layer_id], "dp", axis=0, tiled=True),
            lax.all_gather(w_inner[layer_id], "dp", axis=1, tiled=True),
            lax.all_gather(w_outer[layer_id], "dp", axis=1, tiled=True),
        )
        fetched.append(weights)
        route_row = expert_ids[layer_id].reshape(seq_count * block_len)
        stream, saved_state = layer_forward(
            stream, weights, table_full, rel_buckets, route_row, head_count, experts_all, capacity
        )
        kept_states.append(saved_state)
    block_output = stream.astype(jnp.bfloat16)
    grad_stream = out_cotangent.astype(jnp.float32)
    attn_parts = [None] * layer_count
    expert_parts = [None] * layer_count
    table_grad = jnp.zeros(table_full.shape, jnp.float32)
    for layer_id in reversed(range(layer_count)):
        weights = (
            lax.all_gather(gain_attn[layer_id], "dp", axis=0, tiled=True),
            lax.all_gather(w_query[layer_id], "dp", axis=0, tiled=True),
            lax.all_gather(w_key[layer_id], "dp", axis=0, tiled=True),
            lax.all_gather(w_value[layer_id], "dp", axis=0, tiled=True),
            lax.all_gather(w_output[layer_id], "dp", axis=0, tiled=True),
            lax.all_gather(gain_ffn[layer_id], "dp", axis=0, tiled=True),
            lax.all_gather(w_router[layer_id], "dp", axis=0, tiled=True),
            lax.all_gather(w_inner[layer_id], "dp", axis=1, tiled=True),
            lax.all_gather(w_outer[layer_id], "dp", axis=1, tiled=True),
        )
        grad_stream, attn_terms, expert_terms, table_part = layer_backward(
            grad_stream,
            kept_states[layer_id],
            weights,
            table_full,
            rel_buckets,
            head_count,
            experts_all,
            capacity,
        )
        attn_parts[layer_id] = attn_terms
        expert_parts[layer_id] = expert_terms
        table_grad = table_grad + table_part
    gain_one_all = stack_member(attn_parts, 0)
    query_all = stack_member(attn_parts, 1)
    key_all = stack_member(attn_parts, 2)
    value_all = stack_member(attn_parts, 3)
    output_all = stack_member(attn_parts, 4)
    gain_two_all = stack_member(attn_parts, 5)
    router_all = stack_member(attn_parts, 6)
    inner_all = stack_member(expert_parts, 0)
    outer_all = stack_member(expert_parts, 1)
    reduced = (
        lax.psum_scatter(
            gain_one_all.astype(jnp.bfloat16), "dp", scatter_dimension=1, tiled=True
        ).astype(jnp.float32),
        lax.psum_scatter(
            query_all.astype(jnp.bfloat16), "dp", scatter_dimension=1, tiled=True
        ).astype(jnp.float32),
        lax.psum_scatter(
            key_all.astype(jnp.bfloat16), "dp", scatter_dimension=1, tiled=True
        ).astype(jnp.float32),
        lax.psum_scatter(
            value_all.astype(jnp.bfloat16), "dp", scatter_dimension=1, tiled=True
        ).astype(jnp.float32),
        lax.psum_scatter(
            output_all.astype(jnp.bfloat16), "dp", scatter_dimension=1, tiled=True
        ).astype(jnp.float32),
        lax.psum_scatter(
            gain_two_all.astype(jnp.bfloat16), "dp", scatter_dimension=1, tiled=True
        ).astype(jnp.float32),
        lax.psum_scatter(
            router_all.astype(jnp.bfloat16), "dp", scatter_dimension=1, tiled=True
        ).astype(jnp.float32),
        lax.psum_scatter(
            table_grad.astype(jnp.bfloat16), "dp", scatter_dimension=1, tiled=True
        ).astype(jnp.float32),
        lax.psum_scatter(
            inner_all.astype(jnp.bfloat16), "dp", scatter_dimension=2, tiled=True
        ).astype(jnp.float32),
        lax.psum_scatter(
            outer_all.astype(jnp.bfloat16), "dp", scatter_dimension=2, tiled=True
        ).astype(jnp.float32),
    )
    summed = (
        lax.psum(reduced[0].astype(jnp.bfloat16), ("ctx", "exp")).astype(jnp.float32),
        lax.psum(reduced[1].astype(jnp.bfloat16), ("ctx", "exp")).astype(jnp.float32),
        lax.psum(reduced[2].astype(jnp.bfloat16), ("ctx", "exp")).astype(jnp.float32),
        lax.psum(reduced[3].astype(jnp.bfloat16), ("ctx", "exp")).astype(jnp.float32),
        lax.psum(reduced[4].astype(jnp.bfloat16), ("ctx", "exp")).astype(jnp.float32),
        lax.psum(reduced[5].astype(jnp.bfloat16), ("ctx", "exp")).astype(jnp.float32),
        lax.psum(reduced[6].astype(jnp.bfloat16), ("ctx", "exp")).astype(jnp.float32),
        lax.psum(reduced[7].astype(jnp.bfloat16), ("ctx", "exp")).astype(jnp.float32),
    )
    inner_sum, outer_sum = (
        lax.psum(reduced[8].astype(jnp.bfloat16), "ctx").astype(jnp.float32),
        lax.psum(reduced[9].astype(jnp.bfloat16), "ctx").astype(jnp.float32),
    )
    return (
        block_output,
        grad_stream,
        summed[0],
        summed[1],
        summed[2],
        summed[3],
        summed[4],
        summed[5],
        summed[6],
        inner_sum,
        outer_sum,
        summed[7],
    )


def solution(mesh):
    in_specs = (
        P(("dp", "exp"), "ctx", None),
        P(("dp", "exp"), "ctx", None),
        P(None, ("dp", "exp"), "ctx", None, None),
        P(),
        P(),
        P(None, "dp"),
        P(None, "dp", None),
        P(None, "dp", None),
        P(None, "dp", None),
        P(None, "dp", None),
        P(None, "dp"),
        P(None, "dp", None),
        P(None, "exp", "dp", None),
        P(None, "exp", "dp", None),
    )
    out_specs = (
        P(("dp", "exp"), "ctx", None),
        P(("dp", "exp"), "ctx", None),
        P(None, "dp"),
        P(None, "dp", None),
        P(None, "dp", None),
        P(None, "dp", None),
        P(None, "dp", None),
        P(None, "dp"),
        P(None, "dp", None),
        P(None, "exp", "dp", None),
        P(None, "exp", "dp", None),
        P(None, "dp"),
    )
    return jax.shard_map(shards, mesh=mesh, in_specs=in_specs, out_specs=out_specs, check_vma=False)
```

profile of v0, /device:TPU:0, one launch (start us, length us, event | category | flops | bytes accessed | tf_op | source)
XLA Modules:
  0.0 1827.7 jit_solution(10851303832899626659)
XLA Ops:
  13.1 4.9 fusion.277
  18.1 5.0 fusion.278
  29.5 9.1 all-reduce.8
  96.7 75.2 %while.106 = (s32[]{:T(128)}, bf16[1,256,768]{1,2,0:T(8,128)(2,1)}, bf16[1,256,768]{1,2,0:T(8,128)(2,1)}, f32[1,12,256]{2,1,0:T(8,128)S(1)}, f32[1,12,256]{2,1,0...) while((s32[]{:T(128)}, bf16[1,256,768]{1,2,0:T(8,128)(2,1)}, ...), condition=%wide.region_6.7_spmd, body=%wide.region_3.6_spmd.sunk | while | flops 511321120 | bytes 40537144 | solution.py:109
  183.1 11.0 all-gather.6
  195.1 9.1 all-gather.15
  205.7 8.5 fusion.104
  214.2 10.0 all-gather.41.cloned.1.call-done
  224.2 8.5 fusion.147
  238.9 10.6 all-to-all-done.1
  270.5 10.9 all-gather.47.cloned.1.call-done
  289.3 79.9 %while.107 = (s32[]{:T(128)}, bf16[1,256,768]{1,2,0:T(8,128)(2,1)}, bf16[1,256,768]{1,2,0:T(8,128)(2,1)}, f32[1,12,256]{2,1,0:T(8,128)S(1)}, f32[1,12,256]{2,1,0...) while((s32[]{:T(128)}, bf16[1,256,768]{1,2,0:T(8,128)(2,1)}, ...), condition=%wide.region_21.22_spmd, body=%wide.region_18.21_spmd.sunk | while | flops 511321120 | bytes 40530964 | solution.py:109
  306.0 5.3 collective-permute-done.3
  394.1 6.8 all-to-all-done.4
  403.0 8.5 fusion.96
  411.5 20.4 %all-gather.53.cloned.1.call-done = bf16[1,2,3072,768]{3,2,1,0:T(8,128)(2,1)} async-done(((bf16[1,2,768,768]{3,2,1,0:T(8,128)(2,1)}), bf16[1,2,3072,768]{3,2,1,0:T(8,128)(2,1)}) %all-gather.53.cloned.1.call-update) | async-done | bytes 9437200 | tf_op jit(solution)/shard_map/all_gather | solution.py:436
  431.8 8.8 fusion.120
  448.6 8.5 fusion.153
  468.7 5.6 all-to-all-done.3
  487.0 167.8 %while.108 = (s32[]{:T(128)}, bf16[1,256,768]{1,2,0:T(8,128)(2,1)}, bf16[1,256,768]{1,2,0:T(8,128)(2,1)}, f32[1,256,12,64]{1,3,2,0:T(8,128)}, f32[1,256,12,64]{1...) while((s32[]{:T(128)}, bf16[1,256,768]{1,2,0:T(8,128)(2,1)}, ...), condition=%wide.region_35.36_spmd.clone, body=%wide.region_34.35_spmd.clone.sunk | while | flops 1121321728 | bytes 72032424 | solution.py:168
  515.9 6.2 fusion.433
  559.3 6.2 fusion.433
  600.6 6.2 fusion.433
  641.9 6.2 fusion.433
  668.2 7.9 all-to-all-done.6
  676.2 9.1 fusion.113
  707.6 165.6 %while.109 = (s32[]{:T(128)}, bf16[1,256,768]{1,2,0:T(8,128)(2,1)}, bf16[1,256,768]{1,2,0:T(8,128)(2,1)}, f32[1,256,12,64]{1,3,2,0:T(8,128)}, f32[1,256,12,64]{1...) while((s32[]{:T(128)}, bf16[1,256,768]{1,2,0:T(8,128)(2,1)}, ...), condition=%wide.region_42.43_spmd.clone, body=%wide.region_41.42_spmd.clone.sunk | while | flops 1121321728 | bytes 72032424 | solution.py:168
  736.5 6.2 fusion.449
  777.6 6.2 fusion.449
  818.9 6.2 fusion.449
  860.3 6.2 fusion.449
  889.7 4.8 convert_bitcast_fusion.2
  899.4 8.1 pad_maximum_fusion
  908.6 10.3 convert_bitcast_fusion
  919.0 10.3 convert_bitcast_fusion.1
  929.3 16.9 pad_maximum_fusion.1
  954.2 25.5 %reduce-scatter.20.cloned.1.call-done = bf16[2,192,768]{2,1,0:T(8,128)(2,1)} async-done(((bf16[2,768,768]{2,1,0:T(8,128)(2,1)}), bf16[2,192,768]{2,1,0:T(8,128)(2,1)}) %reduce-scatter.20.cloned.1.call-update) | async-done | bytes 589840 | tf_op jit(solution)/shard_map/reduce_scatter | solution.py:493
  979.6 35.7 %reduce-scatter.22.cloned.1.call-done = bf16[2,192,768]{2,1,0:T(8,128)(2,1)} async-done(((bf16[2,768,768]{2,1,0:T(8,128)(2,1)}), bf16[2,192,768]{2,1,0:T(8,128)(2,1)}) %reduce-scatter.22.cloned.1.call-update) | async-done | bytes 589840 | tf_op jit(solution)/shard_map/reduce_scatter | solution.py:496
  1015.4 141.9 %reduce-scatter.24.cloned.1.call-done = bf16[2,2,192,3072]{3,2,1,0:T(8,128)(2,1)} async-done(((bf16[2,2,768,3072]{3,2,1,0:T(8,128)(2,1)}), bf16[2,2,192,3072]{3,2,1,0:T(8,128)(2,1)}) %reduce-scatter.24.cloned.1.call-update) | async-done | bytes 4718608 | tf_op jit(solution)/shard_map/reduce_scatter | solution.py:508
  1157.2 142.1 %reduce-scatter.26.cloned.1.call-done = bf16[2,2,768,768]{3,2,1,0:T(8,128)(2,1)} async-done(((bf16[2,2,3072,768]{3,2,1,0:T(8,128)(2,1)}), bf16[2,2,768,768]{3,2,1,0:T(8,128)(2,1)}) %reduce-scatter.26.cloned.1.call-update) | async-done | bytes 4718608 | tf_op jit(solution)/shard_map/reduce_scatter | solution.py:511
  1300.0 22.1 %reduce-scatter.32.cloned.1.call-done = bf16[192,8]{1,0:T(8,128)(2,1)} async-done(((bf16[768,8]{1,0:T(8,128)(2,1)}), bf16[192,8]{1,0:T(8,128)(2,1)}) %reduce-scatter.32.cloned.1.call-update) | async-done | bytes 3088
  1323.1 5.8 all-reduce.4
  1330.1 14.7 reduce-scatter.28.cloned.1.call-done
  1345.7 21.9 %reduce-scatter.30.cloned.1.call-done = bf16[192,2]{1,0:T(8,128)(2,1)} async-done(((bf16[768,2]{1,0:T(8,128)(2,1)}), bf16[192,2]{1,0:T(8,128)(2,1)}) %reduce-scatter.30.cloned.1.call-update) | async-done | bytes 784
  1368.4 22.2 %all-reduce.5 = (bf16[2,192]{1,0:T(2,128)(2,1)S(1)}, bf16[2,192]{1,0:T(2,128)(2,1)S(1)}, bf16[2,192,4]{1,2,0:T(4,128)(2,1)S(1)}, bf16[32,3]{0,1:T(4,128)(2,1)S(1)}) all-reduce(bf16[2,192]{1,0:T(2,128)(2,1)S(1)} %copy.251, bf16[2,192]{1,0:T(2,128)(2,1)S(1)} %copy.253, ...), channel_id=1, replica_groups=mesh['dp'=4,'ctx'=4,'exp'=2] {'ctx','exp'}, use_global_device_ids=true, to_apply=%region_47.48 | all-reduce | flops 2400 | bytes 9600 | tf_op jit(solution)/shard_map/psum | solution.py:516
  1393.0 88.7 %all-reduce.12.cloned.1.call-done = (bf16[2,192,768]{2,1,0:T(8,128)(2,1)}, bf16[2,192,768]{2,1,0:T(8,128)(2,1)}, bf16[2,192,768]{2,1,0:T(8,128)(2,1)}, bf16[2,192,768]{2,1,0:T(8,128)(2,1)}) async-done(((bf16[2,192,768]{2,1,0:T(8,128)(2,1)}, bf16[2,192,768]{2,1,0:T(8,128)(2,1)}, bf16[2,192,768]{2,1,0:T(8,128)(2,1)}, bf16[2,192,768]{2,1,0:T(8,128)(2,1)}), (bf16[2,192,768]{2,1,0:T(8,128)(2,1)}, ...) | async-done | bytes 2359312 | tf_op jit(solution)/shard_map/psum | solution.py:517
  1488.3 320.5 %all-reduce.14.cloned.1.call-done = (bf16[2,2,192,3072]{3,2,1,0:T(8,128)(2,1)}, bf16[2,2,768,768]{3,2,1,0:T(8,128)(2,1)}) async-done(((bf16[2,2,192,3072]{3,2,1,0:T(8,128)(2,1)}, bf16[2,2,768,768]{3,2,1,0:T(8,128)(2,1)}), (bf16[2,2,192,3072]{3,2,1,0:T(8,128)(2,1)}, bf16[2,2,768,768]{3,2,1,0:T(8,128)(2,1)})) %all-reduce.14.cloned.1.call-update) | async-done | bytes 9437200 | tf_op jit(solution)/shard_map/psum | solution.py:526
  1808.9 7.5 convert_element_type.657
  (1027 shorter events, 689.6 us)
Async XLA Ops:
  7.2 65.3 %all-gather.31.cloned.1.call-start = ((), (), s32[]{:S(2)}) async-start(), calls=%async_computation.23 | async-start | bytes 1474560 | tf_op jit(solution)/shard_map/all_gather | solution.py:430
  9.3 71.4 %all-gather.33.cloned.1.call-start = ((), (), s32[]{:S(2)}) async-start(), calls=%async_computation.24 | async-start | bytes 1474560 | tf_op jit(solution)/shard_map/all_gather | solution.py:431
  11.2 77.5 %all-gather.35.cloned.1.call-start = ((), (), s32[]{:S(2)}) async-start(), calls=%async_computation.25 | async-start | bytes 1474560 | tf_op jit(solution)/shard_map/all_gather | solution.py:429
  12.2 162.1 %all-gather.37.cloned.1.call-start = ((), (), s32[]{:S(2)}) async-start(), calls=%async_computation.26 | async-start | bytes 1474560 | tf_op jit(solution)/shard_map/all_gather | solution.py:432
  13.1 192.6 %all-gather.39.cloned.1.call-start = ((), (), s32[]{:S(2)}) async-start(), calls=%async_computation.27 | async-start | bytes 11796480 | tf_op jit(solution)/shard_map/all_gather | solution.py:435
  18.0 206.2 %all-gather.41.cloned.1.call-start = ((), (), s32[]{:S(2)}) async-start(), calls=%async_computation.28 | async-start | bytes 11796480 | tf_op jit(solution)/shard_map/all_gather | solution.py:436
  23.1 229.0 %all-gather.43.cloned.1.call-start = ((), (), s32[]{:S(2)}) async-start(), calls=%async_computation.29 | async-start | bytes 1474560 | tf_op jit(solution)/shard_map/all_gather | solution.py:430
  23.9 238.5 %all-gather.45.cloned.1.call-start = ((), (), s32[]{:S(2)}) async-start(), calls=%async_computation.30 | async-start | bytes 1474560 | tf_op jit(solution)/shard_map/all_gather | solution.py:431
  24.6 256.8 %all-gather.47.cloned.1.call-start = ((), (), s32[]{:S(2)}) async-start(), calls=%async_computation.31 | async-start | bytes 1474560 | tf_op jit(solution)/shard_map/all_gather | solution.py:429
  25.3 345.8 %all-gather.49.cloned.1.call-start = ((), (), s32[]{:S(2)}) async-start(), calls=%async_computation.32 | async-start | bytes 1474560 | tf_op jit(solution)/shard_map/all_gather | solution.py:432
  25.9 377.0 %all-gather.51.cloned.1.call-start = ((), (), s32[]{:S(2)}) async-start(), calls=%async_computation.33 | async-start | bytes 11796480 | tf_op jit(solution)/shard_map/all_gather | solution.py:435
  26.7 405.2 %all-gather.53.cloned.1.call-start = ((), (), s32[]{:S(2)}) async-start(), calls=%async_computation.34 | async-start | bytes 11796480 | tf_op jit(solution)/shard_map/all_gather | solution.py:436
  98.6 18.6 %collective-permute-start.1 = (bf16[1,256,768]{1,2,0:T(8,128)(2,1)}, bf16[1,256,768]{1,2,0:T(8,128)(2,1)}, u32[]{:S(2)}, u32[]{:S(2)}) collective-permute-start(bf16[1,256,768]{1,2,0:T(8,128)(2,1)} %get-tuple-element.2333), channel_id=1, source_target_pairs={{6,0},{0,2},{2,4},{4,6},{7,1},{1,3},{3,5},{5,7},{14,8},{8,10},{10,... | collective-permute-start | bytes 1179656 | tf_op jit(solution)/shard_map/while/body/eval_jaxpr/ppermute | solution.py:15
  122.9 19.3 %collective-permute-start.1 = (bf16[1,256,768]{1,2,0:T(8,128)(2,1)}, bf16[1,256,768]{1,2,0:T(8,128)(2,1)}, u32[]{:S(2)}, u32[]{:S(2)}) collective-permute-start(bf16[1,256,768]{1,2,0:T(8,128)(2,1)} %get-tuple-element.2333), channel_id=1, source_target_pairs={{6,0},{0,2},{2,4},{4,6},{7,1},{1,3},{3,5},{5,7},{14,8},{8,10},{10,... | collective-permute-start | bytes 1179656 | tf_op jit(solution)/shard_map/while/body/eval_jaxpr/ppermute | solution.py:15
  147.9 18.4 %collective-permute-start.1 = (bf16[1,256,768]{1,2,0:T(8,128)(2,1)}, bf16[1,256,768]{1,2,0:T(8,128)(2,1)}, u32[]{:S(2)}, u32[]{:S(2)}) collective-permute-start(bf16[1,256,768]{1,2,0:T(8,128)(2,1)} %get-tuple-element.2333), channel_id=1, source_target_pairs={{6,0},{0,2},{2,4},{4,6},{7,1},{1,3},{3,5},{5,7},{14,8},{8,10},{10,... | collective-permute-start | bytes 1179656 | tf_op jit(solution)/shard_map/while/body/eval_jaxpr/ppermute | solution.py:15
  179.3 26.3 %all-to-all-start = ((bf16[4,128,768]{2,1,0:T(8,128)(2,1)}), bf16[4,128,768]{2,1,0:T(8,128)(2,1)S(1)}, u32[]{:S(2)}, u32[]{:S(2)}) async-start(bf16[4,128,768]{2,1,0:T(8,128)(2,1)} %bitcast.793), calls=%async_computation | async-start | bytes 1572864 | tf_op jit(solution)/shard_map/all_to_all | solution.py:227
  291.0 20.3 %collective-permute-start.3 = (bf16[1,256,768]{1,2,0:T(8,128)(2,1)}, bf16[1,256,768]{1,2,0:T(8,128)(2,1)}, u32[]{:S(2)}, u32[]{:S(2)}) collective-permute-start(bf16[1,256,768]{1,2,0:T(8,128)(2,1)} %get-tuple-element.2384), channel_id=1, source_target_pairs={{6,0},{0,2},{2,4},{4,6},{7,1},{1,3},{3,5},{5,7},{14,8},{8,10},{10,... | collective-permute-start | bytes 1179656 | tf_op jit(solution)/shard_map/while/body/eval_jaxpr/ppermute | solution.py:15
  317.0 21.0 %collective-permute-start.3 = (bf16[1,256,768]{1,2,0:T(8,128)(2,1)}, bf16[1,256,768]{1,2,0:T(8,128)(2,1)}, u32[]{:S(2)}, u32[]{:S(2)}) collective-permute-start(bf16[1,256,768]{1,2,0:T(8,128)(2,1)} %get-tuple-element.2384), channel_id=1, source_target_pairs={{6,0},{0,2},{2,4},{4,6},{7,1},{1,3},{3,5},{5,7},{14,8},{8,10},{10,... | collective-permute-start | bytes 1179656 | tf_op jit(solution)/shard_map/while/body/eval_jaxpr/ppermute | solution.py:15
  343.6 20.0 %collective-permute-start.3 = (bf16[1,256,768]{1,2,0:T(8,128)(2,1)}, bf16[1,256,768]{1,2,0:T(8,128)(2,1)}, u32[]{:S(2)}, u32[]{:S(2)}) collective-permute-start(bf16[1,256,768]{1,2,0:T(8,128)(2,1)} %get-tuple-element.2384), channel_id=1, source_target_pairs={{6,0},{0,2},{2,4},{4,6},{7,1},{1,3},{3,5},{5,7},{14,8},{8,10},{10,... | collective-permute-start | bytes 1179656 | tf_op jit(solution)/shard_map/while/body/eval_jaxpr/ppermute | solution.py:15
  489.2 41.6 %collective-permute-start.4 = (bf16[1,256,768]{1,2,0:T(8,128)(2,1)}, bf16[1,256,768]{1,2,0:T(8,128)(2,1)}, u32[]{:S(2)}, u32[]{:S(2)}) collective-permute-start(bf16[1,256,768]{1,2,0:T(8,128)(2,1)} %copy.326), channel_id=1, source_target_pairs={{6,0},{0,2},{2,4},{4,6},{7,1},{1,3},{3,5},{5,7},{14,8},{8,10},{10,... | collective-permute-start | bytes 1179656 | tf_op jit(solution)/shard_map/while/body/eval_jaxpr/ppermute | solution.py:15
  492.5 38.4 %collective-permute-start.5 = (bf16[1,256,768]{1,2,0:T(8,128)(2,1)}, bf16[1,256,768]{1,2,0:T(8,128)(2,1)}, u32[]{:S(2)}, u32[]{:S(2)}) collective-permute-start(bf16[1,256,768]{1,2,0:T(8,128)(2,1)} %copy.327), channel_id=1, source_target_pairs={{6,0},{0,2},{2,4},{4,6},{7,1},{1,3},{3,5},{5,7},{14,8},{8,10},{10,... | collective-permute-start | bytes 1179656 | tf_op jit(solution)/shard_map/while/body/eval_jaxpr/ppermute | solution.py:15
  532.6 39.5 %collective-permute-start.4 = (bf16[1,256,768]{1,2,0:T(8,128)(2,1)}, bf16[1,256,768]{1,2,0:T(8,128)(2,1)}, u32[]{:S(2)}, u32[]{:S(2)}) collective-permute-start(bf16[1,256,768]{1,2,0:T(8,128)(2,1)} %copy.326), channel_id=1, source_target_pairs={{6,0},{0,2},{2,4},{4,6},{7,1},{1,3},{3,5},{5,7},{14,8},{8,10},{10,... | collective-permute-start | bytes 1179656 | tf_op jit(solution)/shard_map/while/body/eval_jaxpr/ppermute | solution.py:15
  534.4 37.8 %collective-permute-start.5 = (bf16[1,256,768]{1,2,0:T(8,128)(2,1)}, bf16[1,256,768]{1,2,0:T(8,128)(2,1)}, u32[]{:S(2)}, u32[]{:S(2)}) collective-permute-start(bf16[1,256,768]{1,2,0:T(8,128)(2,1)} %copy.327), channel_id=1, source_target_pairs={{6,0},{0,2},{2,4},{4,6},{7,1},{1,3},{3,5},{5,7},{14,8},{8,10},{10,... | collective-permute-start | bytes 1179656 | tf_op jit(solution)/shard_map/while/body/eval_jaxpr/ppermute | solution.py:15
  550.4 17.8 collective-permute-start.6
  574.0 39.5 %collective-permute-start.4 = (bf16[1,256,768]{1,2,0:T(8,128)(2,1)}, bf16[1,256,768]{1,2,0:T(8,128)(2,1)}, u32[]{:S(2)}, u32[]{:S(2)}) collective-permute-start(bf16[1,256,768]{1,2,0:T(8,128)(2,1)} %copy.326), channel_id=1, source_target_pairs={{6,0},{0,2},{2,4},{4,6},{7,1},{1,3},{3,5},{5,7},{14,8},{8,10},{10,... | collective-permute-start | bytes 1179656 | tf_op jit(solution)/shard_map/while/body/eval_jaxpr/ppermute | solution.py:15
  575.7 37.8 %collective-permute-start.5 = (bf16[1,256,768]{1,2,0:T(8,128)(2,1)}, bf16[1,256,768]{1,2,0:T(8,128)(2,1)}, u32[]{:S(2)}, u32[]{:S(2)}) collective-permute-start(bf16[1,256,768]{1,2,0:T(8,128)(2,1)} %copy.327), channel_id=1, source_target_pairs={{6,0},{0,2},{2,4},{4,6},{7,1},{1,3},{3,5},{5,7},{14,8},{8,10},{10,... | collective-permute-start | bytes 1179656 | tf_op jit(solution)/shard_map/while/body/eval_jaxpr/ppermute | solution.py:15
  592.0 17.6 collective-permute-start.6
  615.3 39.5 %collective-permute-start.4 = (bf16[1,256,768]{1,2,0:T(8,128)(2,1)}, bf16[1,256,768]{1,2,0:T(8,128)(2,1)}, u32[]{:S(2)}, u32[]{:S(2)}) collective-permute-start(bf16[1,256,768]{1,2,0:T(8,128)(2,1)} %copy.326), channel_id=1, source_target_pairs={{6,0},{0,2},{2,4},{4,6},{7,1},{1,3},{3,5},{5,7},{14,8},{8,10},{10,... | collective-permute-start | bytes 1179656 | tf_op jit(solution)/shard_map/while/body/eval_jaxpr/ppermute | solution.py:15
  617.1 37.7 %collective-permute-start.5 = (bf16[1,256,768]{1,2,0:T(8,128)(2,1)}, bf16[1,256,768]{1,2,0:T(8,128)(2,1)}, u32[]{:S(2)}, u32[]{:S(2)}) collective-permute-start(bf16[1,256,768]{1,2,0:T(8,128)(2,1)} %copy.327), channel_id=1, source_target_pairs={{6,0},{0,2},{2,4},{4,6},{7,1},{1,3},{3,5},{5,7},{14,8},{8,10},{10,... | collective-permute-start | bytes 1179656 | tf_op jit(solution)/shard_map/while/body/eval_jaxpr/ppermute | solution.py:15
  693.3 260.9 %reduce-scatter.16.cloned.1.call-start = ((), (), s32[]{:S(2)}) async-start(), calls=%async_computation.17 | async-start | bytes 2949120 | tf_op jit(solution)/shard_map/reduce_scatter | solution.py:487
  709.8 39.3 %collective-permute-start.8 = (bf16[1,256,768]{1,2,0:T(8,128)(2,1)}, bf16[1,256,768]{1,2,0:T(8,128)(2,1)}, u32[]{:S(2)}, u32[]{:S(2)}) collective-permute-start(bf16[1,256,768]{1,2,0:T(8,128)(2,1)} %copy.347), channel_id=1, source_target_pairs={{6,0},{0,2},{2,4},{4,6},{7,1},{1,3},{3,5},{5,7},{14,8},{8,10},{10,... | collective-permute-start | bytes 1179656 | tf_op jit(solution)/shard_map/while/body/eval_jaxpr/ppermute | solution.py:15
  711.6 37.6 %collective-permute-start.9 = (bf16[1,256,768]{1,2,0:T(8,128)(2,1)}, bf16[1,256,768]{1,2,0:T(8,128)(2,1)}, u32[]{:S(2)}, u32[]{:S(2)}) collective-permute-start(bf16[1,256,768]{1,2,0:T(8,128)(2,1)} %copy.348), channel_id=1, source_target_pairs={{6,0},{0,2},{2,4},{4,6},{7,1},{1,3},{3,5},{5,7},{14,8},{8,10},{10,... | collective-permute-start | bytes 1179656 | tf_op jit(solution)/shard_map/while/body/eval_jaxpr/ppermute | solution.py:15
  750.9 39.6 %collective-permute-start.8 = (bf16[1,256,768]{1,2,0:T(8,128)(2,1)}, bf16[1,256,768]{1,2,0:T(8,128)(2,1)}, u32[]{:S(2)}, u32[]{:S(2)}) collective-permute-start(bf16[1,256,768]{1,2,0:T(8,128)(2,1)} %copy.347), channel_id=1, source_target_pairs={{6,0},{0,2},{2,4},{4,6},{7,1},{1,3},{3,5},{5,7},{14,8},{8,10},{10,... | collective-permute-start | bytes 1179656 | tf_op jit(solution)/shard_map/while/body/eval_jaxpr/ppermute | solution.py:15
  752.7 37.8 %collective-permute-start.9 = (bf16[1,256,768]{1,2,0:T(8,128)(2,1)}, bf16[1,256,768]{1,2,0:T(8,128)(2,1)}, u32[]{:S(2)}, u32[]{:S(2)}) collective-permute-start(bf16[1,256,768]{1,2,0:T(8,128)(2,1)} %copy.348), channel_id=1, source_target_pairs={{6,0},{0,2},{2,4},{4,6},{7,1},{1,3},{3,5},{5,7},{14,8},{8,10},{10,... | collective-permute-start | bytes 1179656 | tf_op jit(solution)/shard_map/while/body/eval_jaxpr/ppermute | solution.py:15
  792.3 39.6 %collective-permute-start.8 = (bf16[1,256,768]{1,2,0:T(8,128)(2,1)}, bf16[1,256,768]{1,2,0:T(8,128)(2,1)}, u32[]{:S(2)}, u32[]{:S(2)}) collective-permute-start(bf16[1,256,768]{1,2,0:T(8,128)(2,1)} %copy.347), channel_id=1, source_target_pairs={{6,0},{0,2},{2,4},{4,6},{7,1},{1,3},{3,5},{5,7},{14,8},{8,10},{10,... | collective-permute-start | bytes 1179656 | tf_op jit(solution)/shard_map/while/body/eval_jaxpr/ppermute | solution.py:15
  794.0 37.8 %collective-permute-start.9 = (bf16[1,256,768]{1,2,0:T(8,128)(2,1)}, bf16[1,256,768]{1,2,0:T(8,128)(2,1)}, u32[]{:S(2)}, u32[]{:S(2)}) collective-permute-start(bf16[1,256,768]{1,2,0:T(8,128)(2,1)} %copy.348), channel_id=1, source_target_pairs={{6,0},{0,2},{2,4},{4,6},{7,1},{1,3},{3,5},{5,7},{14,8},{8,10},{10,... | collective-permute-start | bytes 1179656 | tf_op jit(solution)/shard_map/while/body/eval_jaxpr/ppermute | solution.py:15
  833.6 39.6 %collective-permute-start.8 = (bf16[1,256,768]{1,2,0:T(8,128)(2,1)}, bf16[1,256,768]{1,2,0:T(8,128)(2,1)}, u32[]{:S(2)}, u32[]{:S(2)}) collective-permute-start(bf16[1,256,768]{1,2,0:T(8,128)(2,1)} %copy.347), channel_id=1, source_target_pairs={{6,0},{0,2},{2,4},{4,6},{7,1},{1,3},{3,5},{5,7},{14,8},{8,10},{10,... | collective-permute-start | bytes 1179656 | tf_op jit(solution)/shard_map/while/body/eval_jaxpr/ppermute | solution.py:15
  835.4 37.8 %collective-permute-start.9 = (bf16[1,256,768]{1,2,0:T(8,128)(2,1)}, bf16[1,256,768]{1,2,0:T(8,128)(2,1)}, u32[]{:S(2)}, u32[]{:S(2)}) collective-permute-start(bf16[1,256,768]{1,2,0:T(8,128)(2,1)} %copy.348), channel_id=1, source_target_pairs={{6,0},{0,2},{2,4},{4,6},{7,1},{1,3},{3,5},{5,7},{14,8},{8,10},{10,... | collective-permute-start | bytes 1179656 | tf_op jit(solution)/shard_map/while/body/eval_jaxpr/ppermute | solution.py:15
  878.5 75.6 %reduce-scatter.18.cloned.1.call-start = ((), (), s32[]{:S(2)}) async-start(), calls=%async_computation.18 | async-start | bytes 2949120 | tf_op jit(solution)/shard_map/reduce_scatter | solution.py:490
  882.7 96.9 %reduce-scatter.20.cloned.1.call-start = ((), (), s32[]{:S(2)}) async-start(), calls=%async_computation.19 | async-start | bytes 2949120 | tf_op jit(solution)/shard_map/reduce_scatter | solution.py:493
  886.3 129.0 %reduce-scatter.22.cloned.1.call-start = ((), (), s32[]{:S(2)}) async-start(), calls=%async_computation.20 | async-start | bytes 2949120 | tf_op jit(solution)/shard_map/reduce_scatter | solution.py:496
  889.7 267.6 %reduce-scatter.24.cloned.1.call-start = ((), (), s32[]{:S(2)}) async-start(), calls=%async_computation.21 | async-start | bytes 23592960 | tf_op jit(solution)/shard_map/reduce_scatter | solution.py:508
  907.5 391.8 %reduce-scatter.26.cloned.1.call-start = ((), (), s32[]{:S(2)}) async-start(), calls=%async_computation.22 | async-start | bytes 23592960 | tf_op jit(solution)/shard_map/reduce_scatter | solution.py:511
  946.2 375.9 %reduce-scatter.32.cloned.1.call-start = ((), (), s32[]{:S(2)}) async-start(), calls=%async_computation.37 | async-start | bytes 245760
  948.9 395.9 %reduce-scatter.28.cloned.1.call-start = ((), (), s32[]{:S(2)}) async-start(), calls=%async_computation.35 | async-start | bytes 245760
  953.1 414.4 %reduce-scatter.30.cloned.1.call-start = ((), (), s32[]{:S(2)}) async-start(), calls=%async_computation.36 | async-start | bytes 245760
  954.1 527.6 %all-reduce.12.cloned.1.call-start = ((), (), s32[]{:S(2)}) async-start(), calls=%async_computation.38 | async-start | bytes 4718592 | tf_op jit(solution)/shard_map/psum | solution.py:517
  1015.3 793.5 %all-reduce.14.cloned.1.call-start = ((), (), s32[]{:S(2)}) async-start(), calls=%async_computation.39 | async-start | bytes 18874368 | tf_op jit(solution)/shard_map/psum | solution.py:526
  (233 other events, 1792.2 us)
Sparse Core Ops, SparseCore 0:
  10.2 20.1 all-gather.30
  32.5 17.4 all-gather.32
  51.6 17.4 all-gather.34
  71.1 17.4 all-gather.36
  90.0 64.2 all-gather.38
  155.7 68.4 all-gather.40
  225.8 17.4 all-gather.42
  244.8 17.4 all-gather.44
  263.9 17.4 all-gather.46
  282.8 17.4 all-gather.48
  301.9 64.2 all-gather.50
  367.6 64.2 all-gather.52
  878.7 29.7 reduce-scatter.15
  911.0 33.0 reduce-scatter.17
  946.6 33.0 reduce-scatter.19
  982.2 33.0 reduce-scatter.21
  1017.7 139.4 reduce-scatter.23
  1159.9 139.4 reduce-scatter.25
  1302.4 19.7 reduce-scatter.31
  1325.0 19.7 reduce-scatter.27
  1347.8 19.7 reduce-scatter.29
  1371.5 110.2 all-reduce.11
  1484.5 324.3 all-reduce.13
where the time goes:
time: 1840 us; the launch traced here: 1830 us
  waiting for transfers between devices  943 us (51%)
  matrix products  334 us (18%)
  local copies, waits for them, and re-layouts  257 us (14%)
  other arithmetic  137 us (7%)
  starting transfers between devices  79 us (4%)
  blocking collectives  57.2 us (3%)
    psum x1, waiting for transfers between devices, shards(): lax.psum(reduced[8].astype(jnp.bfloat16), 'ctx').astype(jnp.float32)  321 us
    reduce_scatter x1, waiting for transfers between devices, shards(): lax.psum_scatter(outer_all.astype(jnp.bfloat16), 'dp', scatter_dimension=...  142 us
    reduce_scatter x1, waiting for transfers between devices, shards(): lax.psum_scatter(inner_all.astype(jnp.bfloat16), 'dp', scatter_dimension=...  142 us
    psum x1, waiting for transfers between devices, shards(): lax.psum(reduced[1].astype(jnp.bfloat16), ('ctx', 'exp'))  88.7 us
    unnamed x26, waiting for transfers between devices  62.8 us
    dot_general x15, matrix products, bias_from_onehot(): jnp.einsum('qkb,bh->hqk', onehot, table_full, precision=PRECISION_HIGH)  62.6 us
    while x168, local copies, waits for them, and re-layouts  58.6 us
    dot_general x15, local copies, waits for them, and re-layouts, bias_from_onehot(): jnp.einsum('qkb,bh->hqk', onehot, table_full, precision=PRECISION_HIGH)  51.8 us
  transfers between devices with their start and end apart: 75, of which 33 were waited for; matrix products, arithmetic and copies ran while one was open for 34% of the time, Pallas kernels for 0%

commit v1 on v0

v1 whole, which is shorter than its diff:
```python
from functools import partial

import jax
import jax.numpy as jnp
from jax import lax
from jax.experimental import pallas as pl
from jax.experimental.pallas import tpu as pltpu
from jax.sharding import PartitionSpec as P

NORM_EPSILON = 1e-06
PRECISION_HIGH = lax.Precision.HIGHEST
LANES = 128
FOLD_ROWS = 8
VMEM_BYTES = 56 * 2**20
F32 = jnp.float32
BF16 = jnp.bfloat16


def rms_norm(values, gain):
    return (
        values * lax.rsqrt(jnp.mean(values * values, axis=-1, keepdims=True) + NORM_EPSILON) * gain
    )


def dot_f32(left, right, dims):
    return lax.dot_general(left, right, (dims, ((), ())), preferred_element_type=F32)


def head_mask(head, head_dim):
    lane = lax.broadcasted_iota(jnp.int32, (1, LANES), 1)
    return (lane >= head * head_dim) & (lane < (head + 1) * head_dim)


def masked(values, mask):
    return jnp.where(mask, values.astype(F32), 0.0).astype(BF16)


def head_scores(query, key, seg_row, scale):
    rows, width = query.shape[0], seg_row.shape[1]
    wide = jnp.broadcast_to(seg_row, (rows, width))
    bias = pltpu.roll(wide, width - (rows - 1), 1, stride=1, stride_axis=0)
    return dot_f32(query, key, ((1,), (1,))) * scale + bias[:, : key.shape[0]]


def forward_kernel(head_dim, seg_ref, query_ref, key_ref, value_ref, out_ref):
    scale = head_dim ** (-0.5)
    query, key, value = query_ref[...], key_ref[...], value_ref[...]
    out = jnp.zeros(out_ref.shape, F32)
    for head in range(LANES // head_dim):
        mask = head_mask(head, head_dim)
        scores = head_scores(masked(query, mask), key, seg_ref[head], scale)
        weights = jnp.exp(scores - jnp.max(scores, axis=-1, keepdims=True))
        total = jnp.sum(weights, axis=-1, keepdims=True)
        mixed = dot_f32(weights.astype(BF16), value, ((1,), (0,))) / total
        out = jnp.where(mask, mixed, out)
    out_ref[...] = out.astype(BF16)


def backward_kernel(
    head_dim, seg_ref, query_ref, key_ref, value_ref, grad_ref, dq_ref, dkv_ref, dseg_ref
):
    scale = head_dim ** (-0.5)
    query, key, value, grad = query_ref[...], key_ref[...], value_ref[...], grad_ref[...]
    rows = query.shape[0]
    dq = jnp.zeros(dq_ref.shape, F32)
    dk = jnp.zeros(key.shape, F32)
    dv = jnp.zeros(key.shape, F32)
    for head in range(LANES // head_dim):
        mask = head_mask(head, head_dim)
        query_h, grad_h = masked(query, mask), masked(grad, mask)
        scores = head_scores(query_h, key, seg_ref[head], scale)
        weights = jnp.exp(scores - jnp.max(scores, axis=-1, keepdims=True))
        probs = weights * (1.0 / jnp.sum(weights, axis=-1, keepdims=True))
        prob_grad = dot_f32(grad_h, value, ((1,), (1,)))
        delta = jnp.sum(probs * prob_grad, axis=-1, keepdims=True)
        score_grad = probs * (prob_grad - delta)
        raw_grad = (score_grad * scale).astype(BF16)
        dq = jnp.where(mask, dot_f32(raw_grad, key, ((1,), (0,))), dq)
        dk = dk + dot_f32(raw_grad, query_h, ((0,), (0,)))
        dv = dv + dot_f32(probs.astype(BF16), grad_h, ((0,), (0,)))
        fold = jnp.concatenate([score_grad, jnp.zeros((rows, rows), F32)], axis=1)
        half = rows // 2
        while half >= FOLD_ROWS:
            fold = pltpu.roll(fold[:half], half, 1) + fold[half:]
            half //= 2
        dseg_ref[head] = fold
    dq_ref[...] = dq.astype(BF16)
    dkv_ref[0] = dk.astype(BF16)
    dkv_ref[1] = dv.astype(BF16)


def attention_specs(rows, span, width, hidden, per_block):
    blocks = hidden // LANES
    return [
        pl.BlockSpec((per_block, 1, width), lambda b: (b, 0, 0)),
        pl.BlockSpec((rows, LANES), lambda b: (0, b)),
        pl.BlockSpec((span, LANES), lambda b: (0, b)),
        pl.BlockSpec((span, LANES), lambda b: (0, b + blocks)),
    ]


def attention_forward(segments, query, keys_values):
    heads, _, width = segments.shape
    rows, hidden = query.shape
    span = keys_values.shape[0]
    head_dim = hidden // heads
    per_block = LANES // head_dim
    return pl.pallas_call(
        partial(forward_kernel, head_dim),
        grid=(hidden // LANES,),
        in_specs=attention_specs(rows, span, width, hidden, per_block),
        out_specs=pl.BlockSpec((rows, LANES), lambda b: (0, b)),
        out_shape=jax.ShapeDtypeStruct((rows, hidden), BF16),
        compiler_params=pltpu.CompilerParams(vmem_limit_bytes=VMEM_BYTES),
        cost_estimate=pl.CostEstimate(
            flops=8 * rows * span * hidden, bytes_accessed=4 * span * hidden, transcendentals=0
        ),
    )(segments, query, keys_values, keys_values)


def attention_backward(segments, query, keys_values, mix_grad):
    heads, _, width = segments.shape
    rows, hidden = query.shape
    span = keys_values.shape[0]
    head_dim = hidden // heads
    per_block = LANES // head_dim
    return pl.pallas_call(
        partial(backward_kernel, head_dim),
        grid=(hidden // LANES,),
        in_specs=attention_specs(rows, span, width, hidden, per_block)
        + [pl.BlockSpec((rows, LANES), lambda b: (0, b))],
        out_specs=[
            pl.BlockSpec((rows, LANES), lambda b: (0, b)),
            pl.BlockSpec((2, span, LANES), lambda b: (0, 0, b)),
            pl.BlockSpec((per_block, FOLD_ROWS, width), lambda b: (b, 0, 0)),
        ],
        out_shape=[
            jax.ShapeDtypeStruct((rows, hidden), BF16),
            jax.ShapeDtypeStruct((2, span, hidden), BF16),
            jax.ShapeDtypeStruct((heads, FOLD_ROWS, width), F32),
        ],
        compiler_params=pltpu.CompilerParams(vmem_limit_bytes=VMEM_BYTES),
        cost_estimate=pl.CostEstimate(
            flops=20 * rows * span * hidden, bytes_accessed=8 * span * hidden, transcendentals=0
        ),
    )(segments, query, keys_values, keys_values, mix_grad)


def dispatch_onehot(ids, first_expert, local_experts, capacity):
    slots = []
    for local in range(local_experts):
        match = (ids == first_expert + local).astype(jnp.int32)
        rank = jnp.cumsum(match, axis=1) - match
        slots.append(jnp.where(match == 1, rank, -1))
    slot = jnp.stack(slots)
    return (
        slot[:, :, None, :] == jnp.arange(capacity, dtype=jnp.int32)[None, None, :, None]
    ).astype(BF16)


def to_experts(onehot, tokens):
    experts, groups, capacity, rows = onehot.shape
    grouped = tokens.reshape(groups, rows, tokens.shape[-1])
    picked = jnp.einsum("egst,gtd->egsd", onehot, grouped, preferred_element_type=F32)
    return picked.astype(BF16).reshape(experts, groups * capacity, tokens.shape[-1])


def to_tokens(onehot, slots):
    experts, groups, capacity, rows = onehot.shape
    grouped = slots.reshape(experts, groups, capacity, slots.shape[-1])
    placed = jnp.einsum("egst,egsd->gtd", onehot, grouped, preferred_element_type=F32)
    return placed.astype(BF16).reshape(groups * rows, slots.shape[-1])


def gather_tokens(rows):
    return lax.all_gather(rows, ("dp", "exp"), axis=0, tiled=True)


def sum_tokens(rows):
    return lax.psum_scatter(rows, ("dp", "exp"), scatter_dimension=0, tiled=True)


def sum_scattered(partial_sum, axes):
    flat = partial_sum.reshape(-1, partial_sum.shape[-1])
    return lax.psum_scatter(flat, axes, scatter_dimension=0, tiled=True)


def shared_sums(own_sums):
    attn_own, inner_own, outer_own = own_sums
    return (
        lax.all_gather(attn_own, ("ctx", "exp"), axis=0, tiled=True),
        lax.all_gather(inner_own, "ctx", axis=0, tiled=True),
        lax.all_gather(outer_own, "ctx", axis=0, tiled=True),
    )


def layer_forward(stream, weights, segments, route_row, onehot, experts_all):
    gain_one, gain_two, router_weight, attn_weight, inner_weight, outer_weight = weights
    width = stream.shape[1]
    normed_one = rms_norm(stream, gain_one).astype(BF16)
    key_value = dot_f32(normed_one, attn_weight[:, width : 3 * width], ((1,), (0,))).astype(BF16)
    keys_values = lax.all_gather(key_value, "ctx", axis=0, tiled=True)
    query = dot_f32(normed_one, attn_weight[:, :width], ((1,), (0,))).astype(BF16)
    mixed = attention_forward(segments, query, keys_values)
    mid = stream + dot_f32(mixed, attn_weight[:, 3 * width :], ((1,), (0,)))
    normed_two = rms_norm(mid, gain_two).astype(BF16)
    tokens = gather_tokens(normed_two)
    router_probs = jax.nn.softmax(dot_f32(normed_two, router_weight, ((1,), (0,))), axis=-1)
    expert_hot = (route_row[:, None] == jnp.arange(experts_all, dtype=jnp.int32)[None, :]).astype(
        F32
    )
    gate = jnp.sum(router_probs * expert_hot, axis=-1, keepdims=True)
    received = to_experts(onehot, tokens)
    pre_act = jnp.einsum("erd,edf->erf", received, inner_weight, preferred_element_type=F32)
    activated = jax.nn.gelu(pre_act, approximate=True).astype(BF16)
    expert_out = jnp.einsum(
        "erf,efd->erd", activated, outer_weight, preferred_element_type=F32
    ).astype(BF16)
    returned = sum_tokens(to_tokens(onehot, expert_out))
    new_stream = mid + gate * returned.astype(F32)
    saved = (
        stream,
        normed_one,
        query,
        keys_values,
        mixed,
        mid,
        normed_two,
        router_probs,
        expert_hot,
        gate,
        received,
        pre_act,
        activated,
        returned,
    )
    return (new_stream, saved)


def layer_backward(grad_stream, saved, weights, segments, onehot, pending):
    gain_one, gain_two, router_weight, attn_weight, inner_weight, outer_weight = weights
    (
        stream,
        normed_one,
        query,
        keys_values,
        mixed,
        mid,
        normed_two,
        router_probs,
        expert_hot,
        gate,
        received,
        pre_act,
        activated,
        returned,
    ) = saved
    width = stream.shape[1]
    out_grad = (gate * grad_stream).astype(BF16)
    expert_grad = to_experts(onehot, gather_tokens(out_grad))
    gate_grad = jnp.sum(grad_stream * returned.astype(F32), axis=-1, keepdims=True)
    act_grad = jnp.einsum("erd,efd->erf", expert_grad, outer_weight, preferred_element_type=F32)
    pre_grad = jax.vjp(partial(jax.nn.gelu, approximate=True), pre_act)[1](act_grad)[0].astype(BF16)
    token_part = jnp.einsum(
        "erf,edf->erd", pre_grad, inner_weight, preferred_element_type=F32
    ).astype(BF16)
    token_back = sum_tokens(to_tokens(onehot, token_part)).astype(F32)
    outer_grad = jnp.einsum(
        "erf,erd->efd", activated, expert_grad, preferred_element_type=F32
    ).astype(BF16)
    inner_grad = jnp.einsum("erd,erf->edf", received, pre_grad, preferred_element_type=F32).astype(
        BF16
    )
    inner_grad = lax.all_to_all(inner_grad, "dp", split_axis=1, concat_axis=2, tiled=True)
    outer_grad = sum_scattered(outer_grad, "ctx")
    inner_grad = sum_scattered(inner_grad, "ctx")
    logit_grad = (router_probs * (expert_hot - gate) * gate_grad).astype(BF16)
    router_grad = dot_f32(normed_two, logit_grad, ((0,), (0,)))
    two_grad = dot_f32(logit_grad, router_weight, ((1,), (1,))) + token_back
    mid_part, gain_two_grad = jax.vjp(rms_norm, mid, gain_two)[1](two_grad)
    mid_grad = grad_stream + mid_part
    attn_grad = mid_grad.astype(BF16)
    mix_grad = dot_f32(attn_grad, attn_weight[:, 3 * width :], ((1,), (1,))).astype(BF16)
    if pending is not None:
        mix_grad, pending = lax.optimization_barrier((mix_grad, pending))
        pending = shared_sums(pending)
    query_grad, key_value_grad, dseg = attention_backward(segments, query, keys_values, mix_grad)
    key_value_grad = lax.psum_scatter(key_value_grad, "ctx", scatter_dimension=1, tiled=True)
    if pending is not None:
        key_value_grad, pending = lax.optimization_barrier((key_value_grad, pending))
    output_grad = dot_f32(mixed, attn_grad, ((0,), (0,))).astype(BF16)
    joined = jnp.concatenate([query_grad, key_value_grad[0], key_value_grad[1]], axis=1)
    qkv_grad = dot_f32(normed_one, joined, ((0,), (0,))).astype(BF16)
    one_grad = dot_f32(joined, attn_weight[:, : 3 * width], ((1,), (1,)))
    attn_weight_grad = lax.psum_scatter(
        jnp.concatenate([qkv_grad, output_grad], axis=1), "dp", scatter_dimension=0, tiled=True
    )
    attn_weight_grad = sum_scattered(attn_weight_grad, ("ctx", "exp"))
    stream_part, gain_one_grad = jax.vjp(rms_norm, stream, gain_one)[1](one_grad)
    small = jnp.concatenate([gain_one_grad[:, None], gain_two_grad[:, None], router_grad], axis=1)
    sums = (attn_weight_grad, inner_grad, outer_grad)
    return (mid_grad + stream_part, sums, pending, small, dseg)


def shards(
    block_input,
    out_cotangent,
    expert_ids,
    rel_buckets,
    bias_table,
    gain_attn,
    w_query,
    w_key,
    w_value,
    w_output,
    gain_ffn,
    w_router,
    w_inner,
    w_outer,
):
    layer_count = gain_attn.shape[0]
    bucket_count, head_count = bias_table.shape
    local_experts = w_inner.shape[1]
    experts_all = local_experts * lax.axis_size("exp")
    rows, width = block_input.shape[0] * block_input.shape[1], block_input.shape[2]
    capacity = 2 * rows // experts_all
    span = rows * lax.axis_size("ctx")
    ctx_index, dp_index = lax.axis_index("ctx"), lax.axis_index("dp")
    shard_rows = w_query.shape[1]

    attn_full = [
        lax.all_gather(
            jnp.concatenate([w_query[l], w_key[l], w_value[l], w_output[l]], axis=1),
            "dp",
            axis=0,
            tiled=True,
        )
        for l in range(layer_count)
    ]
    vectors = lax.all_gather(
        jnp.concatenate([gain_attn[..., None], gain_ffn[..., None], w_router], axis=2),
        "dp",
        axis=1,
        tiled=True,
    )
    ids_all = lax.all_gather(
        expert_ids.reshape(layer_count, 1, rows), ("dp", "exp"), axis=1, tiled=True
    )
    inner_full = [
        lax.all_to_all(w_inner[l], "dp", split_axis=2, concat_axis=1, tiled=True)
        for l in range(layer_count)
    ]

    seg_len = span + rows - 1
    seg_ids = lax.dynamic_slice_in_dim(rel_buckets, span - rows - ctx_index * rows, seg_len)
    seg_ids = jnp.concatenate([seg_ids, jnp.full((1,), -1, jnp.int32)])
    seg_hot = (seg_ids[None, :] == jnp.arange(bucket_count, dtype=jnp.int32)[:, None]).astype(F32)
    segments = jnp.einsum(
        "bh,bm->hm", bias_table.astype(F32), seg_hot, precision=PRECISION_HIGH
    )[:, None, :]

    first_expert = lax.axis_index("exp") * local_experts
    onehots = [
        dispatch_onehot(ids_all[l], first_expert, local_experts, capacity)
        for l in range(layer_count)
    ]
    weights = [
        (
            vectors[l, :, 0].astype(F32),
            vectors[l, :, 1].astype(F32),
            vectors[l, :, 2:],
            attn_full[l],
            inner_full[l],
            w_outer[l],
        )
        for l in range(layer_count)
    ]
    stream = block_input.reshape(rows, width).astype(F32)
    kept = []
    for l in range(layer_count):
        stream, saved = layer_forward(
            stream, weights[l], segments, expert_ids[l].reshape(rows), onehots[l], experts_all
        )
        kept.append(saved)
    block_output = stream.astype(BF16).reshape(block_input.shape)

    grad_stream = out_cotangent.reshape(rows, width).astype(F32)
    shared = [None] * layer_count
    smalls = [None] * layer_count
    dseg8 = jnp.zeros((), F32)
    pending = None
    for l in reversed(range(layer_count)):
        grad_stream, sums, done, smalls[l], dseg_part = layer_backward(
            grad_stream, kept[l], weights[l], segments, onehots[l], pending
        )
        if done is not None:
            shared[l + 1] = done
        pending = sums
        dseg8 = dseg8 + dseg_part
    shared[0] = shared_sums(pending)
    attn_grads = jnp.stack([part[0] for part in shared]).astype(F32)
    inner_grads = jnp.stack([part[1].reshape(w_inner.shape[1:]) for part in shared]).astype(F32)
    outer_grads = jnp.stack([part[2].reshape(w_outer.shape[1:]) for part in shared]).astype(F32)
    small = jnp.stack(smalls)
    dseg = sum(jnp.roll(dseg8[:, i, :], FOLD_ROWS - 1 - i, axis=-1) for i in range(FOLD_ROWS))
    table_grad = jnp.einsum("bm,hm->bh", seg_hot, dseg, precision=PRECISION_HIGH)
    flat = lax.psum(
        jnp.concatenate([small.reshape(-1), table_grad.reshape(-1)]), ("dp", "ctx", "exp")
    )
    small = lax.dynamic_slice_in_dim(
        flat[: small.size].reshape(small.shape), dp_index * shard_rows, shard_rows, axis=1
    )
    heads_local = head_count // lax.axis_size("dp")
    table_grad = lax.dynamic_slice_in_dim(
        flat[-table_grad.size :].reshape(table_grad.shape),
        dp_index * heads_local,
        heads_local,
        axis=1,
    )
    return (
        block_output,
        grad_stream.reshape(block_input.shape),
        small[:, :, 0],
        attn_grads[:, :, :width],
        attn_grads[:, :, width : 2 * width],
        attn_grads[:, :, 2 * width : 3 * width],
        attn_grads[:, :, 3 * width :],
        small[:, :, 1],
        small[:, :, 2:],
        inner_grads,
        outer_grads,
        table_grad,
    )


def solution(mesh):
    in_specs = (
        P(("dp", "exp"), "ctx", None),
        P(("dp", "exp"), "ctx", None),
        P(None, ("dp", "exp"), "ctx", None, None),
        P(),
        P(),
        P(None, "dp"),
        P(None, "dp", None),
        P(None, "dp", None),
        P(None, "dp", None),
        P(None, "dp", None),
        P(None, "dp"),
        P(None, "dp", None),
        P(None, "exp", "dp", None),
        P(None, "exp", "dp", None),
    )
    out_specs = (
        P(("dp", "exp"), "ctx", None),
        P(("dp", "exp"), "ctx", None),
        P(None, "dp"),
        P(None, "dp", None),
        P(None, "dp", None),
        P(None, "dp", None),
        P(None, "dp", None),
        P(None, "dp"),
        P(None, "dp", None),
        P(None, "exp", "dp", None),
        P(None, "exp", "dp", None),
        P(None, "dp"),
    )
    return jax.shard_map(shards, mesh=mesh, in_specs=in_specs, out_specs=out_specs, check_vma=False)
```

time: 1840 us -> 1640 us (0.89)
  matrix products: 334 us -> 134 us
  local copies, waits for them, and re-layouts: 257 us -> 83.1 us
  blocking collectives: 57.2 us -> 197 us
  waiting for transfers between devices: 943 us -> 1080 us
  other arithmetic: 137 us -> 60.3 us
  starting transfers between devices: 79 us -> 10.3 us
  Pallas kernels: 0 us -> 55.3 us
    psum x2 -> x0, waiting for transfers between devices: 409 us -> none  [the longest x1 321 us: shards(): lax.psum(reduced[8].astype(jnp.bfloat16), 'ctx').astype(jnp.float32)]
    all_gather x12 -> x14, waiting for transfers between devices: 46.1 us -> 445 us  [the longest x2 120 us: layer_forward(): keys_values = lax.all_gather(key_value, 'ctx', axis=0, tiled=True)]
    reduce_scatter x6 -> x14, waiting for transfers between devices: 345 us -> 597 us  [the longest x6 319 us: sum_scattered(): return lax.psum_scatter(flat, axes, scatter_dimension=0, tiled=True)]
    dot_general x111 -> x32, matrix products: 256 us -> 76.9 us  [the longest x20 39.2 us: dot_f32(): lax.dot_general(left, right, (dims, ((), ())), preferred_element_type=F32)]
    all_to_all x0 -> x2, blocking collectives: none -> 91.3 us  [layer_backward(): lax.all_to_all(inner_grad, 'dp', split_axis=1, concat_axis=2, tiled=True)]
    while x172 -> x0, local copies, waits for them, and re-layouts: 65.3 us -> none
    unnamed x26 -> x28, waiting for transfers between devices: 62.8 us -> 2.8 us
    pallas_call x0 -> x4, Pallas kernels: none -> 55.3 us  [the longest x2 35.1 us: attention_backward(): pl.pallas_call(partial(backward_kernel, head_dim), grid=(hidden // LANES,...]
  transfers between devices with their start and end apart: 75 -> 30, of which waited for: 33 -> 25; matrix products, arithmetic and copies ran while one was open for 34% -> 11% of each run, Pallas kernels for 0% -> 1%
where the time goes in v1:
time: 1640 us; the launch traced here: 1630 us
  waiting for transfers between devices  1080 us (66%)
  blocking collectives  197 us (12%)
  matrix products  134 us (8%)
  local copies, waits for them, and re-layouts  83.1 us (5%)
  other arithmetic  60.3 us (4%)
  Pallas kernels  55.3 us (3%)
    reduce_scatter x6, waiting for transfers between devices, sum_scattered(): return lax.psum_scatter(flat, axes, scatter_dimension=0, tiled=True)  319 us
    reduce_scatter x4, waiting for transfers between devices, sum_tokens(): lax.psum_scatter(rows, ('dp', 'exp'), scatter_dimension=0, tiled=True)  155 us
    reduce_scatter x2, waiting for transfers between devices, layer_backward(): lax.psum_scatter(key_value_grad, 'ctx', scatter_dimension=1, tiled=True)  122 us
    all_gather x2, waiting for transfers between devices, layer_forward(): keys_values = lax.all_gather(key_value, 'ctx', axis=0, tiled=True)  120 us
    all_gather x2, waiting for transfers between devices, shared_sums(): lax.all_gather(inner_own, 'ctx', axis=0, tiled=True)  94.9 us
    all_to_all x2, blocking collectives, layer_backward(): lax.all_to_all(inner_grad, 'dp', split_axis=1, concat_axis=2, tiled=True)  91.3 us
    all_gather x2, waiting for transfers between devices, shards(): lax.all_gather(jnp.concatenate([w_query[l], w_key[l], w_value[l], w_outpu...  59.6 us
    all_gather x4, waiting for transfers between devices, gather_tokens(): return lax.all_gather(rows, ('dp', 'exp'), axis=0, tiled=True)  58.3 us
  transfers between devices with their start and end apart: 30, of which 25 were waited for; matrix products, arithmetic and copies ran while one was open for 11% of the time, Pallas kernels for 1%

profile of v1, /device:TPU:0, one launch (start us, length us, event | category | flops | bytes accessed | tf_op | source)
XLA Modules:
  0.0 1633.9 jit_solution(13277215810805318670)
XLA Ops:
  13.8 7.9 all_gather.48
  22.4 9.1 fusion.89
  31.5 21.5 %all-gather.16.cloned.1.call-done = bf16[768,3072]{1,0:T(8,128)(2,1)} async-done(((bf16[192,3072]{1,0:T(8,128)(2,1)}), bf16[768,3072]{1,0:T(8,128)(2,1)}) %all-gather.16.cloned.1.call-update) | async-done | bytes 4718608 | tf_op jit(solution)/shard_map/all_gather | solution.py:332
  61.1 59.0 %all-gather.18.cloned.1.call-done.key_ref.value_ref = bf16[1024,1536]{1,0:T(8,128)(2,1)} async-done(((bf16[256,1536]{1,0:T(8,128)(2,1)}), bf16[1024,1536]{1,0:T(8,128)(2,1)}) %all-gather.18.cloned.1.call-update) | async-done | bytes 3145744 | tf_op jit(solution)/shard_map/all_gather | solution.py:202
  120.2 10.1 shard_map.229
  134.0 4.3 fusion.168
  138.3 5.6 copy.300
  147.8 55.0 %all-gather = s32[2,8,1,256,1]{3,0,4,2,1:T(2,128)S(1)} all-gather(s32[2,1,1,256,1]{3,0,4,2,1:T(2,128)S(1)} %copy.236), channel_id=2, replica_groups=mesh['dp'=4,'ctx'=4,'exp'=2] {'dp','exp'}, dimensions={1}, use_global_device_ids=true | all-gather | bytes 18432 | tf_op jit(solution)/shard_map/all_gather | solution.py:346
  215.4 5.5 copy.242
  242.6 39.4 %reduce-scatter.15.cloned.1.call-done = bf16[256,768]{1,0:T(8,128)(2,1)} async-done(((bf16[2048,768]{1,0:T(8,128)(2,1)}), bf16[256,768]{1,0:T(8,128)(2,1)}) %reduce-scatter.15.cloned.1.call-update) | async-done | bytes 393232 | tf_op jit(solution)/shard_map/reduce_scatter | solution.py:180
  283.5 38.0 %all-gather.22.cloned.1.call-done = bf16[768,3072]{1,0:T(8,128)(2,1)} async-done(((bf16[192,3072]{1,0:T(8,128)(2,1)}), bf16[768,3072]{1,0:T(8,128)(2,1)}) %all-gather.22.cloned.1.call-update) | async-done | bytes 4718608 | tf_op jit(solution)/shard_map/all_gather | solution.py:332
  327.7 60.9 %all-gather.24.cloned.1.call-done.key_ref.value_ref = bf16[1024,1536]{1,0:T(8,128)(2,1)} async-done(((bf16[256,1536]{1,0:T(8,128)(2,1)}), bf16[1024,1536]{1,0:T(8,128)(2,1)}) %all-gather.24.cloned.1.call-update) | async-done | bytes 3145744 | tf_op jit(solution)/shard_map/all_gather | solution.py:202
  388.6 10.1 shard_map.230
  402.4 8.6 copy.302
  426.7 33.4 %all-to-all-done.1 = bf16[2,192,3072]{1,0,2:T(2,128)(2,1)S(1)} async-done(((bf16[2,192,3072]{1,0,2:T(2,128)(2,1)}), bf16[2,192,3072]{1,0,2:T(2,128)(2,1)S(1)}, u32[]{:S(2)}, u32[]{:S(2)}) %all-to-all-start.1) | async-done | bytes 2359328 | tf_op jit(solution)/shard_map/all_to_all | solution.py:350
  460.1 5.3 copy.250
  484.0 41.3 %reduce-scatter.17.cloned.1.call-done = bf16[256,768]{1,0:T(8,128)(2,1)} async-done(((bf16[2048,768]{1,0:T(8,128)(2,1)}), bf16[256,768]{1,0:T(8,128)(2,1)}) %reduce-scatter.17.cloned.1.call-update) | async-done | bytes 393232 | tf_op jit(solution)/shard_map/reduce_scatter | solution.py:180
  528.3 32.2 %all-gather.28.cloned.1.call-done = bf16[2048,768]{1,0:T(8,128)(2,1)} async-done(((bf16[256,768]{1,0:T(8,128)(2,1)}), bf16[2048,768]{1,0:T(8,128)(2,1)}) %all-gather.28.cloned.1.call-update) | async-done | bytes 3145744 | tf_op jit(solution)/shard_map/all_gather | solution.py:176
  564.7 9.6 fusion.13
  580.4 45.7 %reduce-scatter.19.cloned.1.call-done = bf16[256,768]{1,0:T(8,128)(2,1)} async-done(((bf16[2048,768]{1,0:T(8,128)(2,1)}), bf16[256,768]{1,0:T(8,128)(2,1)}) %reduce-scatter.19.cloned.1.call-update) | async-done | bytes 393232 | tf_op jit(solution)/shard_map/reduce_scatter | solution.py:180
  632.9 17.6 %shard_map.231 = (bf16[256,768]{1,0:T(8,128)(2,1)}, bf16[2,1024,768]{2,1,0:T(8,128)(2,1)}, f32[12,8,1280]{2,1,0:T(8,128)}) custom-call(f32[12,1,1280]{2,1,0:T(1,128)} %broadcast_in_dim.29.seg_ref, bf16[256,768]{1,0:T(8,128)(2,1)} %convolution_convert_fusion.14.query_ref, bf16[1024,1536]{1,0:T(8,128)(2,1)} %all-gather.24.cloned.1.call-done.key_ref.value_ref, ...), custom_call_target="tpu_custom_call" | custom-call | flops 4026531840 | bytes 6291456 | tf_op jit(solution)/shard_map/pallas_call | solution.py:127
  650.6 60.3 %reduce-scatter.21.cloned.1.call-done = bf16[2,256,768]{2,1,0:T(8,128)(2,1)} async-done(((bf16[2,1024,768]{2,1,0:T(8,128)(2,1)}), bf16[2,256,768]{2,1,0:T(8,128)(2,1)}) %reduce-scatter.21.cloned.1.call-update) | async-done | bytes 786448 | tf_op jit(solution)/shard_map/reduce_scatter | solution.py:288
  724.3 26.1 %all-gather.30.cloned.1.call-done = bf16[2048,768]{1,0:T(8,128)(2,1)} async-done(((bf16[256,768]{1,0:T(8,128)(2,1)}), bf16[2048,768]{1,0:T(8,128)(2,1)}) %all-gather.30.cloned.1.call-update) | async-done | bytes 3145744 | tf_op jit(solution)/shard_map/all_gather | solution.py:176
  754.8 9.2 fusion.6
  769.4 9.9 convolution_convert_fusion.8
  779.6 5.6 convolution_convert_fusion.9
  787.6 37.2 %all_to_all.66 = bf16[2,768,768]{2,0,1:T(2,128)(2,1)S(1)} all-to-all(bf16[2,768,768]{2,0,1:T(2,128)(2,1)S(1)} %copy.260), channel_id=1, replica_groups=mesh['dp'=4,'ctx'=4,'exp'=2] {'dp'}, dimensions={1} | all-to-all | bytes 4718592 | tf_op jit(solution)/shard_map/all_to_all | solution.py:274
  829.5 28.1 %reduce-scatter.23.cloned.1.call-done = bf16[256,768]{1,0:T(8,128)(2,1)} async-done(((bf16[2048,768]{1,0:T(8,128)(2,1)}), bf16[256,768]{1,0:T(8,128)(2,1)}) %reduce-scatter.23.cloned.1.call-update) | async-done | bytes 393232 | tf_op jit(solution)/shard_map/reduce_scatter | solution.py:180
  863.2 44.7 %reduce-scatter.31.cloned.1.call-done = bf16[384,768]{1,0:T(8,128)(2,1)} async-done(((bf16[1536,768]{1,0:T(8,128)(2,1)}), bf16[384,768]{1,0:T(8,128)(2,1)}) %reduce-scatter.31.cloned.1.call-update) | async-done | bytes 589840 | tf_op jit(solution)/shard_map/reduce_scatter | solution.py:185
  907.9 50.4 %reduce-scatter.29.cloned.1.call-done = bf16[96,3072]{1,0:T(8,128)(2,1)} async-done(((bf16[384,3072]{1,0:T(8,128)(2,1)}), bf16[96,3072]{1,0:T(8,128)(2,1)}) %reduce-scatter.29.cloned.1.call-update) | async-done | bytes 589840 | tf_op jit(solution)/shard_map/reduce_scatter | solution.py:185
  958.3 67.1 %reduce-scatter.27.cloned.1.call-done = bf16[24,3072]{1,0:T(8,128)(2,1)} async-done(((bf16[192,3072]{1,0:T(8,128)(2,1)}), bf16[24,3072]{1,0:T(8,128)(2,1)}) %reduce-scatter.27.cloned.1.call-update) | async-done | bytes 147472 | tf_op jit(solution)/shard_map/reduce_scatter | solution.py:185
  1026.9 17.6 %shard_map.232 = (bf16[256,768]{1,0:T(8,128)(2,1)}, bf16[2,1024,768]{2,1,0:T(8,128)(2,1)}, f32[12,8,1280]{2,1,0:T(8,128)}) custom-call(f32[12,1,1280]{2,1,0:T(1,128)} %broadcast_in_dim.29.seg_ref, bf16[256,768]{1,0:T(8,128)(2,1)} %convolution_convert_fusion.15.query_ref, bf16[1024,1536]{1,0:T(8,128)(2,1)} %all-gather.18.cloned.1.call-done.key_ref.value_ref, ...), custom_call_target="tpu_custom_call" | custom-call | flops 4026531840 | bytes 6291456 | tf_op jit(solution)/shard_map/pallas_call | solution.py:127
  1045.9 21.9 %all-gather.32.cloned.1.call-done = bf16[192,3072]{1,0:T(8,128)(2,1)} async-done(((bf16[24,3072]{1,0:T(8,128)(2,1)}), bf16[192,3072]{1,0:T(8,128)(2,1)}) %all-gather.32.cloned.1.call-update) | async-done | bytes 1179664 | tf_op jit(solution)/shard_map/all_gather | solution.py:191
  1067.8 50.9 %all-gather.34.cloned.1.call-done = bf16[384,3072]{1,0:T(8,128)(2,1)} async-done(((bf16[96,3072]{1,0:T(8,128)(2,1)}), bf16[384,3072]{1,0:T(8,128)(2,1)}) %all-gather.34.cloned.1.call-update) | async-done | bytes 2359312 | tf_op jit(solution)/shard_map/all_gather | solution.py:192
  1118.7 50.8 %all-gather.36.cloned.1.call-done = bf16[1536,768]{1,0:T(8,128)(2,1)} async-done(((bf16[384,768]{1,0:T(8,128)(2,1)}), bf16[1536,768]{1,0:T(8,128)(2,1)}) %all-gather.36.cloned.1.call-update) | async-done | bytes 2359312 | tf_op jit(solution)/shard_map/all_gather | solution.py:193
  1169.6 62.1 %reduce-scatter.33.cloned.1.call-done = bf16[2,256,768]{2,1,0:T(8,128)(2,1)} async-done(((bf16[2,1024,768]{2,1,0:T(8,128)(2,1)}), bf16[2,256,768]{2,1,0:T(8,128)(2,1)}) %reduce-scatter.33.cloned.1.call-update) | async-done | bytes 786448 | tf_op jit(solution)/shard_map/reduce_scatter | solution.py:288
  1238.7 9.2 convolution_convert_fusion.6
  1248.0 6.0 convolution_convert_fusion.7
  1256.4 54.1 %all_to_all.67 = bf16[2,768,768]{2,0,1:T(2,128)(2,1)S(1)} all-to-all(bf16[2,768,768]{2,0,1:T(2,128)(2,1)S(1)} %copy.274), channel_id=1, replica_groups=mesh['dp'=4,'ctx'=4,'exp'=2] {'dp'}, dimensions={1} | all-to-all | bytes 4718592 | tf_op jit(solution)/shard_map/all_to_all | solution.py:274
  1315.1 45.7 %reduce-scatter.41.cloned.1.call-done = bf16[384,768]{1,0:T(8,128)(2,1)} async-done(((bf16[1536,768]{1,0:T(8,128)(2,1)}), bf16[384,768]{1,0:T(8,128)(2,1)}) %reduce-scatter.41.cloned.1.call-update) | async-done | bytes 589840 | tf_op jit(solution)/shard_map/reduce_scatter | solution.py:185
  1360.9 50.3 %reduce-scatter.39.cloned.1.call-done = bf16[96,3072]{1,0:T(8,128)(2,1)} async-done(((bf16[384,3072]{1,0:T(8,128)(2,1)}), bf16[96,3072]{1,0:T(8,128)(2,1)}) %reduce-scatter.39.cloned.1.call-update) | async-done | bytes 589840 | tf_op jit(solution)/shard_map/reduce_scatter | solution.py:185
  1416.8 61.1 %reduce-scatter.37.cloned.1.call-done = bf16[24,3072]{1,0:T(8,128)(2,1)} async-done(((bf16[192,3072]{1,0:T(8,128)(2,1)}), bf16[24,3072]{1,0:T(8,128)(2,1)}) %reduce-scatter.37.cloned.1.call-update) | async-done | bytes 147472 | tf_op jit(solution)/shard_map/reduce_scatter | solution.py:185
  1478.9 42.4 %psum.7 = f32[9600]{0:T(1024)S(1)} all-reduce(f32[9600]{0:T(1024)S(1)} %pad_maximum_fusion.12), channel_id=1, replica_groups=mesh['dp'=4,'ctx'=4,'exp'=2] {'dp','ctx','exp'}, use_global_device_ids=true, to_apply=%region_38.39 | all-reduce | flops 9600 | bytes 76800 | tf_op jit(solution)/shard_map/psum | solution.py:407
  1525.8 4.1 all-gather.42.cloned.1.call-done
  1529.9 6.9 maximum_convert_fusion.1
  1536.7 43.9 %all-gather.40.cloned.1.call-done = bf16[384,3072]{1,0:T(8,128)(2,1)} async-done(((bf16[96,3072]{1,0:T(8,128)(2,1)}), bf16[384,3072]{1,0:T(8,128)(2,1)}) %all-gather.40.cloned.1.call-update) | async-done | bytes 2359312 | tf_op jit(solution)/shard_map/all_gather | solution.py:192
  1580.7 6.1 maximum_convert_fusion
  1586.8 36.0 %all-gather.38.cloned.1.call-done = bf16[192,3072]{1,0:T(8,128)(2,1)} async-done(((bf16[24,3072]{1,0:T(8,128)(2,1)}), bf16[192,3072]{1,0:T(8,128)(2,1)}) %all-gather.38.cloned.1.call-update) | async-done | bytes 1179664 | tf_op jit(solution)/shard_map/all_gather | solution.py:191
  (425 shorter events, 189.7 us)
Async XLA Ops:
  7.2 45.9 %all-gather.16.cloned.1.call-start = ((), (), s32[]{:S(2)}) async-start(), calls=%async_computation.18 | async-start | bytes 5898240 | tf_op jit(solution)/shard_map/all_gather | solution.py:332
  12.8 107.4 %all-gather.18.cloned.1.call-start = ((), (), s32[]{:S(2)}) async-start(), calls=%async_computation.19 | async-start | bytes 3932160 | tf_op jit(solution)/shard_map/all_gather | solution.py:202
  56.5 164.4 %all-gather.20.cloned.1.call-start = ((), (), s32[]{:S(2)}) async-start(), calls=%async_computation.20 | async-start | bytes 3538944 | tf_op jit(solution)/shard_map/all_gather | solution.py:176
  143.8 71.5 %all-to-all-start = ((bf16[2,192,3072]{1,0,2:T(2,128)(2,1)}), bf16[2,192,3072]{1,0,2:T(2,128)(2,1)S(1)}, u32[]{:S(2)}, u32[]{:S(2)}) async-start(bf16[2,192,3072]{1,0,2:T(2,128)(2,1)} %bitcast.296), calls=%async_computation | async-start | bytes 6291456 | tf_op jit(solution)/shard_map/all_to_all | solution.py:350
  147.7 134.3 %reduce-scatter.15.cloned.1.call-start = ((), (), s32[]{:S(2)}) async-start(), calls=%async_computation.21 | async-start | bytes 3538944 | tf_op jit(solution)/shard_map/reduce_scatter | solution.py:180
  236.8 84.7 %all-gather.22.cloned.1.call-start = ((), (), s32[]{:S(2)}) async-start(), calls=%async_computation.22 | async-start | bytes 5898240 | tf_op jit(solution)/shard_map/all_gather | solution.py:332
  239.2 149.4 %all-gather.24.cloned.1.call-start = ((), (), s32[]{:S(2)}) async-start(), calls=%async_computation.23 | async-start | bytes 3932160 | tf_op jit(solution)/shard_map/all_gather | solution.py:202
  241.2 83.7 %copy-start.45 = (bf16[1,768,4]{1,2,0:T(4,128)(2,1)}, bf16[1,768,4]{1,2,0:T(4,128)(2,1)S(1)}, u32[]{:S(2)}) copy-start(bf16[1,768,4]{1,2,0:T(4,128)(2,1)S(1)} %copy.235) | copy-start | bytes 18436
  283.3 115.4 %copy-start.5 = (f32[256,768]{1,0:T(8,128)}, f32[256,768]{1,0:T(8,128)S(1)}, u32[]{:S(2)}) copy-start(f32[256,768]{1,0:T(8,128)S(1)} %get-tuple-element.123) | copy-start | bytes 2359300
  324.9 140.5 %all-gather.26.cloned.1.call-start = ((), (), s32[]{:S(2)}) async-start(), calls=%async_computation.24 | async-start | bytes 3538944 | tf_op jit(solution)/shard_map/all_gather | solution.py:176
  411.0 49.0 %all-to-all-start.1 = ((bf16[2,192,3072]{1,0,2:T(2,128)(2,1)}), bf16[2,192,3072]{1,0,2:T(2,128)(2,1)S(1)}, u32[]{:S(2)}, u32[]{:S(2)}) async-start(bf16[2,192,3072]{1,0,2:T(2,128)(2,1)} %bitcast.298), calls=%async_computation.2 | async-start | bytes 6291456 | tf_op jit(solution)/shard_map/all_to_all | solution.py:350
  414.7 110.7 %reduce-scatter.17.cloned.1.call-start = ((), (), s32[]{:S(2)}) async-start(), calls=%async_computation.25 | async-start | bytes 3538944 | tf_op jit(solution)/shard_map/reduce_scatter | solution.py:180
  481.3 79.2 %all-gather.28.cloned.1.call-start = ((), (), s32[]{:S(2)}) async-start(), calls=%async_computation.26 | async-start | bytes 3538944 | tf_op jit(solution)/shard_map/all_gather | solution.py:176
  484.0 80.4 %copy-start.58 = (f32[256]{0:T(256)}, f32[256]{0:T(256)S(1)}, u32[]{:S(2)}) copy-start(f32[256]{0:T(256)S(1)} %get-tuple-element.116) | copy-start | bytes 3076
  528.0 98.1 %reduce-scatter.19.cloned.1.call-start = ((), (), s32[]{:S(2)}) async-start(), calls=%async_computation.27 | async-start | bytes 3538944 | tf_op jit(solution)/shard_map/reduce_scatter | solution.py:180
  579.8 131.1 %reduce-scatter.21.cloned.1.call-start = ((), (), s32[]{:S(2)}) async-start(), calls=%async_computation.28 | async-start | bytes 3932160 | tf_op jit(solution)/shard_map/reduce_scatter | solution.py:288
  650.5 62.3 %copy-start.6 = (f32[256,768]{1,0:T(8,128)S(1)}, f32[256,768]{1,0:T(8,128)}, u32[]{:S(2)}) copy-start(f32[256,768]{1,0:T(8,128)} %copy-done.5) | copy-start | bytes 2359300
  650.5 62.3 %copy-start.48 = (f32[768]{0:T(1024)S(1)}, f32[768]{0:T(1024)}, u32[]{:S(2)}) copy-start(f32[768]{0:T(1024)} %get-tuple-element.111) | copy-start | bytes 9220
  650.5 62.3 %copy-start.78 = (f32[256]{0:T(256)S(1)}, f32[256]{0:T(256)}, u32[]{:S(2)}) copy-start(f32[256]{0:T(256)} %copy-done.77) | copy-start | bytes 3076
  650.5 99.9 %all-gather.30.cloned.1.call-start = ((), (), s32[]{:S(2)}) async-start(), calls=%async_computation.29 | async-start | bytes 3538944 | tf_op jit(solution)/shard_map/all_gather | solution.py:176
  717.9 110.7 %reduce-scatter.25.cloned.1.call-start = ((), (), s32[]{:S(2)}) async-start(), calls=%async_computation.31 | async-start | bytes 5898240 | tf_op jit(solution)/shard_map/reduce_scatter | solution.py:295
  724.3 133.3 %reduce-scatter.23.cloned.1.call-start = ((), (), s32[]{:S(2)}) async-start(), calls=%async_computation.30 | async-start | bytes 3538944 | tf_op jit(solution)/shard_map/reduce_scatter | solution.py:180
  769.4 138.6 %reduce-scatter.31.cloned.1.call-start = ((), (), s32[]{:S(2)}) async-start(), calls=%async_computation.34 | async-start | bytes 2949120 | tf_op jit(solution)/shard_map/reduce_scatter | solution.py:185
  779.4 179.0 %reduce-scatter.29.cloned.1.call-start = ((), (), s32[]{:S(2)}) async-start(), calls=%async_computation.33 | async-start | bytes 2949120 | tf_op jit(solution)/shard_map/reduce_scatter | solution.py:185
  828.6 196.9 %reduce-scatter.27.cloned.1.call-start = ((), (), s32[]{:S(2)}) async-start(), calls=%async_computation.32 | async-start | bytes 1327104 | tf_op jit(solution)/shard_map/reduce_scatter | solution.py:185
  829.2 238.6 %all-gather.32.cloned.1.call-start = ((), (), s32[]{:S(2)}) async-start(), calls=%async_computation.36 | async-start | bytes 1327104 | tf_op jit(solution)/shard_map/all_gather | solution.py:191
  1025.5 93.3 %all-gather.34.cloned.1.call-start = ((), (), s32[]{:S(2)}) async-start(), calls=%async_computation.37 | async-start | bytes 2949120 | tf_op jit(solution)/shard_map/all_gather | solution.py:192
  1026.2 143.3 %all-gather.36.cloned.1.call-start = ((), (), s32[]{:S(2)}) async-start(), calls=%async_computation.38 | async-start | bytes 2949120 | tf_op jit(solution)/shard_map/all_gather | solution.py:193
  1026.8 204.8 %reduce-scatter.33.cloned.1.call-start = ((), (), s32[]{:S(2)}) async-start(), calls=%async_computation.35 | async-start | bytes 3932160 | tf_op jit(solution)/shard_map/reduce_scatter | solution.py:288
  1044.4 189.1 %copy-start.21 = (bf16[1,256,768]{2,1,0:T(8,128)(2,1)S(1)}, bf16[1,256,768]{2,1,0:T(8,128)(2,1)}, u32[]{:S(2)}) copy-start(bf16[1,256,768]{2,1,0:T(8,128)(2,1)} %param.14) | copy-start | bytes 1179652
  1044.4 189.1 %copy-start.54 = (f32[768]{0:T(1024)S(1)}, f32[768]{0:T(1024)}, u32[]{:S(2)}) copy-start(f32[768]{0:T(1024)} %copy-done.53) | copy-start | bytes 9220
  1044.4 189.1 %copy-start.85 = (f32[256]{0:T(256)S(1)}, f32[256]{0:T(256)}, u32[]{:S(2)}) copy-start(f32[256]{0:T(256)} %copy-done.84) | copy-start | bytes 3076
  1044.5 269.9 %reduce-scatter.35.cloned.1.call-start = ((), (), s32[]{:S(2)}) async-start(), calls=%async_computation.39 | async-start | bytes 5898240 | tf_op jit(solution)/shard_map/reduce_scatter | solution.py:295
  1238.7 122.1 %reduce-scatter.41.cloned.1.call-start = ((), (), s32[]{:S(2)}) async-start(), calls=%async_computation.44 | async-start | bytes 2949120 | tf_op jit(solution)/shard_map/reduce_scatter | solution.py:185
  1247.9 163.2 %reduce-scatter.39.cloned.1.call-start = ((), (), s32[]{:S(2)}) async-start(), calls=%async_computation.42 | async-start | bytes 2949120 | tf_op jit(solution)/shard_map/reduce_scatter | solution.py:185
  1314.2 97.0 %copy-start.50 = (bf16[256,4]{0,1:T(4,128)(2,1)S(1)}, bf16[256,4]{0,1:T(4,128)(2,1)}, u32[]{:S(2)}) copy-start(bf16[256,4]{0,1:T(4,128)(2,1)} %copy-done.49) | copy-start | bytes 6148
  1314.2 97.2 %copy-start.60 = (f32[768]{0:T(1024)S(1)}, f32[768]{0:T(1024)}, u32[]{:S(2)}) copy-start(f32[768]{0:T(1024)} %get-tuple-element.104) | copy-start | bytes 9220
  1314.2 97.2 %copy-start.87 = (f32[768]{0:T(1024)S(1)}, f32[768]{0:T(1024)}, u32[]{:S(2)}) copy-start(f32[768]{0:T(1024)} %get-tuple-element.102) | copy-start | bytes 9220
  1314.2 97.3 %copy-start.52 = (bf16[256,4]{0,1:T(4,128)(2,1)S(1)}, bf16[256,4]{0,1:T(4,128)(2,1)}, u32[]{:S(2)}) copy-start(bf16[256,4]{0,1:T(4,128)(2,1)} %copy-done.51) | copy-start | bytes 6148
  1314.2 97.4 %copy-start.61 = (f32[768]{0:T(1024)S(1)}, f32[768]{0:T(1024)}, u32[]{:S(2)}) copy-start(f32[768]{0:T(1024)} %get-tuple-element.100) | copy-start | bytes 9220
  1314.2 97.4 %copy-start.31 = (f32[12,8,1280]{2,1,0:T(8,128)S(1)}, f32[12,8,1280]{2,1,0:T(8,128)}, u32[]{:S(2)}) copy-start(f32[12,8,1280]{2,1,0:T(8,128)} %get-tuple-element.35) | copy-start | bytes 1474564
  1314.2 97.4 %copy-start.32 = (f32[12,8,1280]{2,1,0:T(8,128)S(1)}, f32[12,8,1280]{2,1,0:T(8,128)}, u32[]{:S(2)}) copy-start(f32[12,8,1280]{2,1,0:T(8,128)} %get-tuple-element.36) | copy-start | bytes 1474564
  1314.3 163.7 %reduce-scatter.37.cloned.1.call-start = ((), (), s32[]{:S(2)}) async-start(), calls=%async_computation.40 | async-start | bytes 1327104 | tf_op jit(solution)/shard_map/reduce_scatter | solution.py:185
  1315.0 97.7 %copy-start.43 = (s32[1280]{0:T(1024)S(1)}, s32[1280]{0:T(1024)}, u32[]{:S(2)}) copy-start(s32[1280]{0:T(1024)} %copy-done.42) | copy-start | bytes 15364
  1315.0 214.8 %all-gather.42.cloned.1.call-start = ((), (), s32[]{:S(2)}) async-start(), calls=%async_computation.45 | async-start | bytes 2949120 | tf_op jit(solution)/shard_map/all_gather | solution.py:193
  1360.8 219.8 %all-gather.40.cloned.1.call-start = ((), (), s32[]{:S(2)}) async-start(), calls=%async_computation.43 | async-start | bytes 2949120 | tf_op jit(solution)/shard_map/all_gather | solution.py:192
  1411.2 211.6 %all-gather.38.cloned.1.call-start = ((), (), s32[]{:S(2)}) async-start(), calls=%async_computation.41 | async-start | bytes 1327104 | tf_op jit(solution)/shard_map/all_gather | solution.py:191
  1416.8 107.8 %copy-start.69 = (f32[256]{0:T(256)S(1)}, f32[256]{0:T(256)}, u32[]{:S(2)}) copy-start(f32[256]{0:T(256)} %copy-done.68) | copy-start | bytes 3076
  (84 other events, 1178.7 us)
Sparse Core Ops, SparseCore 0:
  12.9 40.1 all-gather.15
  56.6 63.5 all-gather.17
  134.1 39.3 all-gather.19
  236.9 45.0 reduce-scatter.14
  284.1 37.4 all-gather.21
  325.0 63.4 all-gather.23
  402.6 39.6 all-gather.25
  481.4 43.9 reduce-scatter.16
  528.2 32.3 all-gather.27
  579.9 46.2 reduce-scatter.18
  650.7 60.2 reduce-scatter.20
  718.0 32.3 all-gather.29
  753.1 54.1 reduce-scatter.24
  810.5 47.0 reduce-scatter.22
  859.9 48.0 reduce-scatter.30
  910.8 47.5 reduce-scatter.28
  961.9 63.4 reduce-scatter.26
  1027.7 40.0 all-gather.31
  1069.5 49.2 all-gather.33
  1120.2 49.2 all-gather.35
  1172.5 59.0 reduce-scatter.32
  1238.8 70.5 reduce-scatter.34
  1311.7 49.1 reduce-scatter.40
  1363.5 47.5 reduce-scatter.38
  1414.5 63.4 reduce-scatter.36
  1479.4 50.4 all-gather.41
  1531.3 49.3 all-gather.39
  1582.8 39.8 all-gather.37
